TPU v7x, 128 devices: a whole 4x4x4 slice. The times are simulated.
128 devices in a mesh: seq: 32 (over y, z, core), mp: 4 (over x).
Axes of the slice: x: 4, y: 4, z: 4, core: 2. Of those that a mesh axis runs over, the one named last changes fastest.
Arguments:
- tokens: bfloat16 [65536, 4096], P('seq', 'mp'), may hold values from -6 to 6
- cotangent: bfloat16 [65536, 4096], P('seq', 'mp'), may hold values from -6 to 6
- norm_gain: float32 [4096], replicated, may hold values from 0.5 to 2
- router_weight: float32 [4096], replicated, may hold values from -0.09375 to 0.09375
- w_query: bfloat16 [4096, 2048], P(None, 'mp'), may hold values from -0.09375 to 0.09375
- w_key: bfloat16 [4096, 512], P(None, 'mp'), may hold values from -0.09375 to 0.09375
- w_value: bfloat16 [4096, 512], P(None, 'mp'), may hold values from -0.09375 to 0.09375
- w_out: bfloat16 [2048, 4096], P('mp'), may hold values from -0.125 to 0.125
- routed_index: int32 [32, 512], P('seq'), may hold values from 0 to 2047, as said below
- routed_count: int32 [32], P('seq'), may hold values from 0 to 512, as said below
- routed_dest: int32 [32, 512], P('seq'), may hold values from 0 to 8191, as said below
Outputs:
- input_grad: bfloat16 [65536, 4096], P('seq', 'mp')
Inputs may be any that keep to these rules, and one draw needn't show every extreme that they name: `routed_count`: the counts add up to 8192; in every draw one index of seq has 512 routed tokens and another has none. `routed_index`: for each index of seq the first routed_count entries are distinct local token indices in increasing order; the others are 0. `routed_dest`: place q belongs to compacted owner q // 256, slot q % 256; every place from 0 to 8191 is taken by exactly one routed token, so every owner receives exactly 256. One index of seq sends at most 16 tokens to one owner, and that many in every draw. Within one owner the places follow the sending index of seq, and within one sender the order of its token indices. Entries past routed_count are 0.
All inputs are finite; a program needn't handle non-finite values.
Results may differ from a plain program's by a relative error of at most 0.0039.
Values may be sent and summed in bfloat16 or wider, within the bound.
A program may use at most 128 MiB of HBM per device.

v0:
```python
import jax
import jax.numpy as jnp
from jax import lax
from jax.sharding import PartitionSpec as P

HEAD_DIM = 128
ROUTED_DEV = 256


norm_eps = 1e-05
score_cap = 5.0


def forward_piece(running, query_heads, query_pos, key_rows, value_rows, key_pos):
    numerator, denominator = running
    score_scale = query_heads.shape[-1] ** (-0.5)
    tanh_score = jnp.tanh(
        jnp.einsum("rgd,kd->rgk", query_heads, key_rows, preferred_element_type=jnp.float32)
        * score_scale
        / score_cap
    )
    live_mask = key_pos[None, None, :] <= query_pos[:, None, None]
    weights_un = jnp.where(live_mask, jnp.exp(score_cap * tanh_score), 0.0)
    denominator = denominator + jnp.sum(weights_un, axis=2)
    numerator = numerator + jnp.einsum(
        "rgk,kd->rgd",
        weights_un.astype(jnp.bfloat16),
        value_rows,
        preferred_element_type=jnp.float32,
    )
    return (numerator, denominator)


def score_grads(
    query_heads, query_pos, grad_heads, denominator, row_delta, key_rows, value_rows, key_pos
):
    score_scale = query_heads.shape[-1] ** (-0.5)
    tanh_score = jnp.tanh(
        jnp.einsum("rgd,kd->rgk", query_heads, key_rows, preferred_element_type=jnp.float32)
        * score_scale
        / score_cap
    )
    live_mask = key_pos[None, None, :] <= query_pos[:, None, None]
    prob = jnp.where(live_mask, jnp.exp(score_cap * tanh_score), 0.0) / denominator[:, :, None]
    prob_grad = jnp.einsum(
        "rgd,kd->rgk", grad_heads, value_rows, preferred_element_type=jnp.float32
    )
    raw_grad = prob * (prob_grad - row_delta[:, :, None]) * (1.0 - tanh_score * tanh_score)
    return (prob.astype(jnp.bfloat16), raw_grad.astype(jnp.bfloat16))


def key_terms(prob_round, raw_round, query_heads, grad_heads):
    score_scale = query_heads.shape[-1] ** (-0.5)
    key_part = (
        jnp.einsum("rgk,rgd->kd", raw_round, query_heads, preferred_element_type=jnp.float32)
        * score_scale
    )
    value_part = jnp.einsum(
        "rgk,rgd->kd", prob_round, grad_heads, preferred_element_type=jnp.float32
    )
    return jnp.concatenate([key_part, value_part], axis=1)


def on_device(
    tokens,
    cotangent,
    norm_gain,
    router_weight,
    w_query,
    w_key,
    w_value,
    w_out,
    routed_index,
    routed_count,
    routed_dest,
):
    seq_devices = lax.axis_size("seq")
    tok_rows, quarter = tokens.shape
    owner_rows = ROUTED_DEV
    pair_slots = 2 * owner_rows // seq_devices
    capacity = routed_index.shape[1]
    head_dim = HEAD_DIM
    local_heads = w_query.shape[1] // head_dim
    score_scale = head_dim ** (-0.5)
    model_width = norm_gain.shape[0]
    buffer_rows = seq_devices * pair_slots
    listed = jnp.arange(capacity, dtype=jnp.int32)
    is_valid = listed < routed_count[0]
    local_rows = routed_index[0]
    target = routed_dest[0]
    owner_index = target // owner_rows
    place_slot = target % owner_rows
    pair_hits = jnp.logical_and(
        owner_index[:, None] == jnp.arange(seq_devices, dtype=jnp.int32)[None, :], is_valid[:, None]
    ).astype(jnp.int32)
    pair_rank = jnp.sum(jnp.cumsum(pair_hits, axis=0) * pair_hits, axis=1) - 1
    buffer_place = jnp.where(is_valid, owner_index * pair_slots + pair_rank, buffer_rows)
    source = jnp.zeros((buffer_rows,), jnp.int32).at[buffer_place].set(local_rows, mode="drop")
    filled = jnp.zeros((buffer_rows,), jnp.bool_).at[buffer_place].set(True, mode="drop")
    position = lax.axis_index("seq") * tok_rows + local_rows
    slot_buffer = (
        jnp.full((buffer_rows,), owner_rows, jnp.int32)
        .at[buffer_place]
        .set(place_slot, mode="drop")
    )
    pos_buffer = jnp.zeros((buffer_rows,), jnp.int32).at[buffer_place].set(position, mode="drop")
    row_meta = jnp.stack([slot_buffer, pos_buffer], axis=1)
    send_x = jnp.where(filled[:, None], tokens[source], jnp.zeros((), jnp.bfloat16))
    send_dy = jnp.where(filled[:, None], cotangent[source], jnp.zeros((), jnp.bfloat16))
    got_x, got_dy, got_meta = (
        lax.all_to_all(send_x, "seq", split_axis=0, concat_axis=0, tiled=True),
        lax.all_to_all(send_dy, "seq", split_axis=0, concat_axis=0, tiled=True),
        lax.all_to_all(row_meta, "seq", split_axis=0, concat_axis=0, tiled=True),
    )
    slot_in = got_meta[:, 0]
    compact_x = jnp.zeros((owner_rows, quarter), jnp.bfloat16).at[slot_in].set(got_x, mode="drop")
    compact_dy = jnp.zeros((owner_rows, quarter), jnp.bfloat16).at[slot_in].set(got_dy, mode="drop")
    row_pos = jnp.zeros((owner_rows,), jnp.int32).at[slot_in].set(got_meta[:, 1], mode="drop")
    full_x, full_dy = (
        lax.all_gather(compact_x, "mp", axis=1, tiled=True),
        lax.all_gather(compact_dy, "mp", axis=1, tiled=True),
    )
    x_float = full_x.astype(jnp.float32)
    inv_rms = lax.rsqrt(jnp.mean(x_float * x_float, axis=1) + norm_eps)
    normed = (x_float * inv_rms[:, None] * norm_gain[None, :]).astype(jnp.bfloat16)
    router = jnp.sum(x_float * router_weight[None, :], axis=1)
    queries = jnp.dot(normed, w_query, preferred_element_type=jnp.float32).astype(jnp.bfloat16)
    key_rows = jnp.dot(normed, w_key, preferred_element_type=jnp.float32).astype(jnp.bfloat16)
    value_rows = jnp.dot(normed, w_value, preferred_element_type=jnp.float32).astype(jnp.bfloat16)
    all_keys, all_values, all_pos = (
        lax.all_gather(key_rows, "seq", axis=0, tiled=True),
        lax.all_gather(value_rows, "seq", axis=0, tiled=True),
        lax.all_gather(row_pos, "seq", axis=0, tiled=True),
    )
    key_count = all_keys.shape[0]
    key_block = min(512, key_count)
    block_count = key_count // key_block
    key_blocks = all_keys.reshape(block_count, key_block, head_dim)
    value_blocks = all_values.reshape(block_count, key_block, head_dim)
    pos_blocks = all_pos.reshape(block_count, key_block)
    query_heads = queries.reshape(owner_rows, local_heads, head_dim)

    def forward_step(running, pieces):
        return (forward_piece(running, query_heads, row_pos, pieces[0], pieces[1], pieces[2]), None)

    start_state = (
        jnp.zeros((owner_rows, local_heads, head_dim), jnp.float32),
        jnp.zeros((owner_rows, local_heads), jnp.float32),
    )
    (numerator, denominator), _ = lax.scan(
        forward_step, start_state, (key_blocks, value_blocks, pos_blocks)
    )
    attended = (numerator / denominator[:, :, None]).astype(jnp.bfloat16)
    block_out = jnp.dot(
        attended.reshape(owner_rows, local_heads * head_dim),
        w_out,
        preferred_element_type=jnp.float32,
    )
    dy_float = full_dy.astype(jnp.float32)
    router_part = jnp.sum(dy_float * block_out, axis=1)
    out_grad = (router[:, None] * dy_float).astype(jnp.bfloat16)
    att_grad = lax.dot_general(
        out_grad, w_out, (((1,), (1,)), ((), ())), preferred_element_type=jnp.float32
    ).astype(jnp.bfloat16)
    grad_heads = att_grad.reshape(owner_rows, local_heads, head_dim)
    row_delta = jnp.sum(grad_heads.astype(jnp.float32) * attended.astype(jnp.float32), axis=2)
    zero_query = jnp.zeros((owner_rows, local_heads, head_dim), jnp.float32)

    def both_step(running, pieces):
        prob_round, raw_round = score_grads(
            query_heads,
            row_pos,
            grad_heads,
            denominator,
            row_delta,
            pieces[0],
            pieces[1],
            pieces[2],
        )
        running = running + jnp.einsum(
            "rgk,kd->rgd", raw_round, pieces[0], preferred_element_type=jnp.float32
        )
        return (running, key_terms(prob_round, raw_round, query_heads, grad_heads))

    query_sum, kv_parts = lax.scan(both_step, zero_query, (key_blocks, value_blocks, pos_blocks))
    kv_grad = lax.psum_scatter(
        kv_parts.reshape(key_count, 2 * head_dim), "seq", scatter_dimension=0, tiled=True
    )
    query_grad = (
        (query_sum * score_scale).astype(jnp.bfloat16).reshape(owner_rows, local_heads * head_dim)
    )
    key_grad = kv_grad[:, :head_dim].astype(jnp.bfloat16)
    value_grad = kv_grad[:, head_dim:].astype(jnp.bfloat16)
    contract = (((1,), (1,)), ((), ()))
    summed = lax.dot_general(w_query, query_grad, contract, preferred_element_type=jnp.float32)
    summed = summed + lax.dot_general(w_key, key_grad, contract, preferred_element_type=jnp.float32)
    summed = summed + lax.dot_general(
        w_value, value_grad, contract, preferred_element_type=jnp.float32
    )
    normed_grad = lax.psum_scatter(
        norm_gain[:, None] * summed, "mp", scatter_dimension=0, tiled=True
    )
    feature_start = lax.axis_index("mp") * quarter
    x_part = lax.dynamic_slice_in_dim(full_x, feature_start, quarter, 1).astype(jnp.float32).T
    router_part_w = lax.dynamic_slice_in_dim(router_weight, feature_start, quarter, 0)
    stat_part = jnp.sum(x_part * normed_grad, axis=0)
    router_grad, stat = lax.psum((router_part, stat_part), "mp")
    branch = (
        inv_rms[None, :] * normed_grad
        - x_part * (inv_rms * inv_rms * inv_rms * stat / model_width)[None, :]
        + router_part_w[:, None] * router_grad[None, :]
    ).astype(jnp.bfloat16)
    pick_cols = jnp.minimum(slot_in, owner_rows - 1)
    back_rows = jnp.where(
        (slot_in < owner_rows)[None, :],
        jnp.take(branch, pick_cols, axis=1),
        jnp.zeros((), jnp.bfloat16),
    )
    returned = lax.all_to_all(back_rows, "seq", split_axis=1, concat_axis=1, tiled=True)
    rows_grad = jnp.take(returned, jnp.minimum(buffer_place, buffer_rows - 1), axis=1).T
    updated = (cotangent[local_rows].astype(jnp.float32) + rows_grad.astype(jnp.float32)).astype(
        jnp.bfloat16
    )
    return cotangent.at[jnp.where(is_valid, local_rows, tok_rows)].set(updated, mode="drop")


def solution(mesh):
    in_specs = (
        P("seq", "mp"),
        P("seq", "mp"),
        P(),
        P(),
        P(None, "mp"),
        P(None, "mp"),
        P(None, "mp"),
        P("mp", None),
        P("seq", None),
        P("seq"),
        P("seq", None),
    )
    out_specs = P("seq", "mp")
    return jax.shard_map(
        on_device, mesh=mesh, in_specs=in_specs, out_specs=out_specs, check_vma=False
    )
```

profile of v0, /device:TPU:1, one launch (start us, length us, event | category | flops | bytes accessed | tf_op | source)
XLA Modules:
  0.0 622.4 jit_solution(12066470707981950804)
XLA Ops:
  6.5 4.8 copy.95
  19.4 9.6 %all-to-all-start = ((s32[32,16,2]{1,2,0:T(2,128)}), s32[32,16,2]{1,2,0:T(2,128)S(1)}, u32[]{:S(2)}, u32[]{:S(2)}) async-start(s32[32,16,2]{1,2,0:T(2,128)} %copy.43), calls=%async_computation | async-start | bytes 65536 | tf_op jit(solution)/shard_map/all_to_all | solution.py:113
  34.0 5.5 gather_fusion
  39.5 5.5 gather_fusion.1
  46.5 7.5 %all-to-all-start.1 = ((bf16[32,16,1024]{2,1,0:T(8,128)(2,1)}), bf16[32,16,1024]{2,1,0:T(8,128)(2,1)S(1)}, u32[]{:S(2)}, u32[]{:S(2)}) async-start(bf16[32,16,1024]{2,1,0:T(8,128)(2,1)} %get-tuple-element.421), calls=%async_computation.1 | async-start | bytes 2097152 | tf_op jit(solution)/shard_map/all_to_all | solution.py:111
  54.6 16.3 %all-to-all-done.1 = bf16[32,16,1024]{2,1,0:T(8,128)(2,1)S(1)} async-done(((bf16[32,16,1024]{2,1,0:T(8,128)(2,1)}), bf16[32,16,1024]{2,1,0:T(8,128)(2,1)S(1)}, u32[]{:S(2)}, u32[]{:S(2)}) %all-to-all-start.1) | async-done | bytes 1048608 | tf_op jit(solution)/shard_map/all_to_all | solution.py:111
  70.9 3.5 scatter_custom_fusion.4
  74.5 20.7 %all_to_all.36 = bf16[32,16,1024]{2,1,0:T(8,128)(2,1)S(1)} all-to-all(bf16[32,16,1024]{2,1,0:T(8,128)(2,1)S(1)} %copy-done.4), channel_id=1, replica_groups=mesh['seq'=32,'mp'=4] {'seq'}, dimensions={0} | all-to-all | bytes 2097152 | tf_op jit(solution)/shard_map/all_to_all | solution.py:112
  95.2 3.4 scatter_custom_fusion.6
  98.7 4.3 all-gather.6.cloned.1.call-done
  112.2 25.0 %all-gather = s32[32,1,256]{2,1,0:T(1,128)S(1)} all-gather(s32[1,1,256]{2,1,0:T(1,128)S(1)} %bitcast.216), channel_id=1, replica_groups=mesh['seq'=32,'mp'=4] {'seq'}, dimensions={0}, use_global_device_ids=true | all-gather | bytes 33792 | tf_op jit(solution)/shard_map/all_gather | solution.py:133
  137.4 4.1 fusion.37
  141.7 4.1 convolution_convert_fusion
  146.0 36.3 %all-gather.10.cloned.1.call-done = bf16[8192,128]{1,0:T(8,128)(2,1)} async-done(((bf16[256,128]{1,0:T(8,128)(2,1)}), bf16[8192,128]{1,0:T(8,128)(2,1)}) %all-gather.10.cloned.1.call-update) | async-done | bytes 2097168 | tf_op jit(solution)/shard_map/all_gather | solution.py:132
  182.2 45.4 %all-gather.8.cloned.1.call-done = bf16[8192,128]{1,0:T(8,128)(2,1)} async-done(((bf16[256,128]{1,0:T(8,128)(2,1)}), bf16[8192,128]{1,0:T(8,128)(2,1)}) %all-gather.8.cloned.1.call-update) | async-done | bytes 2097168 | tf_op jit(solution)/shard_map/all_gather | solution.py:131
  227.6 55.4 %while.30 = (s32[]{:T(128)}, f32[256,4,128]{2,0,1:T(8,128)S(1)}, f32[256,4]{0,1:T(4,128)S(1)}, s32[16,512]{1,0:T(8,128)S(1)}, s32[256]{0:T(256)S(1)}, /*index=5*...) while((s32[]{:T(128)}, f32[256,4,128]{2,0,1:T(8,128)S(1)}, ...), condition=%wide.region_12.13_spmd.clone, body=%wide.region_10.12_spmd.clone.sunk | while | flops 271451136 | bytes 3955844 | solution.py:150
  283.4 118.9 %while.31 = (s32[]{:T(128)}, f32[256,4,128]{2,0,1:T(8,128)S(1)}, f32[16,512,256]{2,1,0:T(8,128)}, s32[16,512]{1,0:T(8,128)S(1)}, s32[256]{0:T(256)S(1)}, /*index...) while((s32[]{:T(128)}, f32[256,4,128]{2,0,1:T(8,128)S(1)}, ...), condition=%wide.region_17.18_spmd.clone, body=%wide.region_16.17_spmd.clone.sunk | while | flops 679542784 | bytes 16010403 | solution.py:185
  402.6 89.8 %reduce-scatter.3.cloned.1.call-done = f32[256,256]{1,0:T(8,128)} async-done(((f32[8192,256]{1,0:T(8,128)}), f32[256,256]{1,0:T(8,128)}) %reduce-scatter.3.cloned.1.call-update) | async-done | bytes 262160 | tf_op jit(solution)/shard_map/reduce_scatter | solution.py:186
  499.8 4.4 fusion.36
  504.1 43.3 %reduce-scatter.5.cloned.1.call-done = f32[1024,256]{0,1:T(8,128)} async-done(((f32[4096,256]{0,1:T(8,128)}), f32[1024,256]{0,1:T(8,128)}) %reduce-scatter.5.cloned.1.call-update) | async-done | bytes 1048592 | tf_op jit(solution)/shard_map/reduce_scatter | solution.py:200
  549.1 6.6 %all-reduce = (f32[256]{0:T(256)S(1)}, f32[256]{0:T(256)S(1)}) all-reduce(f32[256]{0:T(256)S(1)} %fusion.36, f32[256]{0:T(256)S(1)} %fusion.42), channel_id=1, replica_groups=mesh['seq'=32,'mp'=4] {'mp'}, use_global_device_ids=true, to_apply=%region_23.24 | all-reduce | flops 512 | bytes 4096 | tf_op jit(solution)/shard_map/psum | solution.py:207
  560.3 10.0 %all-to-all-start.3 = ((bf16[1024,32,16]{0,2,1:T(8,128)(2,1)}), bf16[1024,32,16]{0,2,1:T(8,128)(2,1)S(1)}, u32[]{:S(2)}, u32[]{:S(2)}) async-start(bf16[1024,32,16]{0,2,1:T(8,128)(2,1)} %select_select_fusion), calls=%async_computation.5 | async-start | bytes 2097152 | tf_op jit(solution)/shard_map/all_to_all | solution.py:219
  570.3 16.8 %all-to-all-done.3 = bf16[1024,32,16]{0,2,1:T(8,128)(2,1)S(1)} async-done(((bf16[1024,32,16]{0,2,1:T(8,128)(2,1)}), bf16[1024,32,16]{0,2,1:T(8,128)(2,1)S(1)}, u32[]{:S(2)}, u32[]{:S(2)}) %all-to-all-start.3) | async-done | bytes 1048608 | tf_op jit(solution)/shard_map/all_to_all | solution.py:219
  587.1 28.1 %scatter_custom_fusion.7 = bf16[2048,1024]{1,0:T(8,128)(2,1)} fusion(bf16[2048,1024]{1,0:T(8,128)(2,1)} %copy.95, s32[512]{0:T(512)S(1)} %bitcast.233, pred[512]{0:T(512)(128)(4,1)S(1)} %compare_and_fusion, bf16[]{:T(256)} %constant.191.clone.1, bf16[1024,512]{0,1:T(8,128)(2,1)S(1)} %bitcast.206, s32[1024]{0:T(1024)S(1)} %pad_clamp_fusion, ...), kind=kCustom, calls=%fused_computation.76 | custom fusion | flops 2621440 | bytes 9445890 | tf_op jit(solution)/shard_map/scatter | solution.py:224
  (340 shorter events, 211.1 us)
Async XLA Ops:
  6.5 101.7 %copy-start = (bf16[4096,128]{1,0:T(8,128)(2,1)S(1)}, bf16[4096,128]{1,0:T(8,128)(2,1)}, u32[]{:S(2)}) copy-start(bf16[4096,128]{1,0:T(8,128)(2,1)} %param.20) | copy-start | bytes 3145732
  6.5 7.1 %copy-start.9 = (s32[1,512]{1,0:T(1,128)S(1)}, s32[1,512]{1,0:T(1,128)}, u32[]{:S(2)}) copy-start(s32[1,512]{1,0:T(1,128)} %param.23) | copy-start | bytes 6148
  6.5 5.4 copy-start.7
  19.4 27.1 %all-to-all-start = ((s32[32,16,2]{1,2,0:T(2,128)}), s32[32,16,2]{1,2,0:T(2,128)S(1)}, u32[]{:S(2)}, u32[]{:S(2)}) async-start(s32[32,16,2]{1,2,0:T(2,128)} %copy.43), calls=%async_computation | async-start | bytes 65536 | tf_op jit(solution)/shard_map/all_to_all | solution.py:113
  46.5 28.0 %copy-start.4 = (bf16[32,16,1024]{2,1,0:T(8,128)(2,1)S(1)}, bf16[32,16,1024]{2,1,0:T(8,128)(2,1)}, u32[]{:S(2)}) copy-start(bf16[32,16,1024]{2,1,0:T(8,128)(2,1)} %get-tuple-element.420) | copy-start | bytes 3145732
  46.5 24.4 %all-to-all-start.1 = ((bf16[32,16,1024]{2,1,0:T(8,128)(2,1)}), bf16[32,16,1024]{2,1,0:T(8,128)(2,1)S(1)}, u32[]{:S(2)}, u32[]{:S(2)}) async-start(bf16[32,16,1024]{2,1,0:T(8,128)(2,1)} %get-tuple-element.421), calls=%async_computation.1 | async-start | bytes 2097152 | tf_op jit(solution)/shard_map/all_to_all | solution.py:111
  54.0 48.9 %all-gather.6.cloned.1.call-start = ((), (), s32[]{:S(2)}) async-start(), calls=%async_computation.6 | async-start | bytes 2621440 | tf_op jit(solution)/shard_map/all_gather | solution.py:120
  70.9 32.0 %copy-start.6 = (f32[4096]{0:T(1024)S(1)}, f32[4096]{0:T(1024)}, u32[]{:S(2)}) copy-start(f32[4096]{0:T(1024)} %param.18) | copy-start | bytes 49156
  74.4 63.0 %all-gather.12.cloned.1.call-start = ((), (), s32[]{:S(2)}) async-start(), calls=%async_computation.9 | async-start | bytes 2621440 | tf_op jit(solution)/shard_map/all_gather | solution.py:121
  95.2 10.3 %copy-start.8 = (f32[4096]{0:T(1024)S(1)}, f32[4096]{0:T(1024)}, u32[]{:S(2)}) copy-start(f32[4096]{0:T(1024)} %param.17) | copy-start | bytes 49156
  98.6 83.6 %all-gather.10.cloned.1.call-start = ((), (), s32[]{:S(2)}) async-start(), calls=%async_computation.8 | async-start | bytes 2162688 | tf_op jit(solution)/shard_map/all_gather | solution.py:132
  102.9 2.6 copy-start.1
  108.2 119.4 %all-gather.8.cloned.1.call-start = ((), (), s32[]{:S(2)}) async-start(), calls=%async_computation.7 | async-start | bytes 2162688 | tf_op jit(solution)/shard_map/all_gather | solution.py:131
  109.7 382.7 %reduce-scatter.3.cloned.1.call-start = ((), (), s32[]{:S(2)}) async-start(), calls=%async_computation.10 | async-start | bytes 8650752 | tf_op jit(solution)/shard_map/reduce_scatter | solution.py:186
  402.2 145.2 %reduce-scatter.5.cloned.1.call-start = ((), (), s32[]{:S(2)}) async-start(), calls=%async_computation.11 | async-start | bytes 5242880 | tf_op jit(solution)/shard_map/reduce_scatter | solution.py:200
  493.3 2.2 copy-start.2
  495.5 1.4 copy-start.5
  499.8 55.9 %dynamic-slice-start = ((f32[4096]{0:T(1024)}, s32[]{:T(128)}), f32[1024]{0:T(1024)S(1)}, s32[]{:S(2)}) async-start(f32[4096]{0:T(1024)} %param.18, s32[]{:T(128)} %select_n.184), calls=%async_computation.12 | async-start | bytes 8704 | tf_op jit(solution)/shard_map/dynamic_slice | solution.py:205
  547.4 8.2 %copy-start.3 = (f32[1024,256]{0,1:T(8,128)S(1)}, f32[1024,256]{0,1:T(8,128)}, u32[]{:S(2)}) copy-start(f32[1024,256]{0,1:T(8,128)} %reduce-scatter.5.cloned.1.call-done) | copy-start | bytes 3145732
  560.3 26.8 %all-to-all-start.3 = ((bf16[1024,32,16]{0,2,1:T(8,128)(2,1)}), bf16[1024,32,16]{0,2,1:T(8,128)(2,1)S(1)}, u32[]{:S(2)}, u32[]{:S(2)}) async-start(bf16[1024,32,16]{0,2,1:T(8,128)(2,1)} %select_select_fusion), calls=%async_computation.5 | async-start | bytes 2097152 | tf_op jit(solution)/shard_map/all_to_all | solution.py:219
Sparse Core Ops, SparseCore 0:
  74.5 28.3 all-gather.5
  104.6 30.8 all-gather.11
  137.7 44.4 all-gather.9
  184.4 43.2 all-gather.7
  402.4 89.9 reduce-scatter.2
  499.7 47.7 reduce-scatter.4
where the time goes:
time: 632 us; the launch traced here: 622 us
  waiting for transfers between devices  252 us (40%)
  matrix products  172 us (27%)
  local copies, waits for them, and re-layouts  57.4 us (9%)
  blocking collectives  52.3 us (8%)
  other arithmetic  44.3 us (7%)
  starting transfers between devices  27.8 us (4%)
  between operations  15 us (2%)
    reduce_scatter x1, waiting for transfers between devices, on_device(): lax.psum_scatter(kv_parts.reshape(key_count, 2 * head_dim), 'seq', scatte...  89.8 us
    all_gather x1, waiting for transfers between devices, on_device(): lax.all_gather(key_rows, 'seq', axis=0, tiled=True)  45.4 us
    reduce_scatter x1, waiting for transfers between devices, on_device(): lax.psum_scatter(norm_gain[:, None] * summed, 'mp', scatter_dimension=0,...  43.3 us
    all_gather x1, waiting for transfers between devices, on_device(): lax.all_gather(value_rows, 'seq', axis=0, tiled=True)  36.3 us
    dot_general x16, matrix products, score_grads(): jnp.einsum('rgd,kd->rgk', grad_heads, value_rows, preferred_element_type=...  31.2 us
    scatter x1, other arithmetic, on_device(): cotangent.at[jnp.where(is_valid, local_rows, tok_rows)]  28.1 us
    dot_general x16, matrix products, forward_piece(): jnp.einsum('rgd,kd->rgk', query_heads, key_rows, preferred_element_type=j...  27.3 us
    all_gather x1, blocking collectives, on_device(): lax.all_gather(row_pos, 'seq', axis=0, tiled=True)  25 us
  transfers between devices with their start and end apart: 9, of which 7 were waited for; matrix products, arithmetic and copies ran while one was open for 7% of the time, Pallas kernels for 0%

commit v1 on v0

v1 whole, which is shorter than its diff:
```python
import functools

import jax
import jax.numpy as jnp
from jax import lax
from jax.experimental import pallas as pl
from jax.experimental.pallas import tpu as pltpu
from jax.sharding import PartitionSpec as P

HEAD_DIM = 128
ROUTED_DEV = 256
KEY_BLOCK = 512

norm_eps = 1e-05
score_cap = 5.0
LOG2E = 1.4426950408889634
SCALE = HEAD_DIM ** (-0.5)

NT = (((1,), (1,)), ((), ()))
NN = (((1,), (0,)), ((), ()))


def dot(a, b, dims=NN):
    return lax.dot_general(a, b, dims, preferred_element_type=jnp.float32)


def live(kpos_row, qpos):
    width = kpos_row.shape[1]
    parts = [kpos_row[:, c : c + 128] <= qpos for c in range(0, width, 128)]
    return jnp.concatenate(parts, axis=1)


def wide(column, width):
    return jnp.concatenate([column] * (width // 128), axis=1)


def forward_kernel(heads, q_ref, qpos_ref, k_ref, v_ref, kpos_ref, att_ref, lden_ref, acc, den):
    step = pl.program_id(0)

    @pl.when(step == 0)
    def _():
        acc[...] = jnp.zeros_like(acc)
        den[...] = jnp.zeros_like(den)

    keys = k_ref[...]
    values = v_ref[...]
    mask = live(kpos_ref[0], qpos_ref[...])
    for h in range(heads):
        cols = slice(h * HEAD_DIM, (h + 1) * HEAD_DIM)
        t = jnp.tanh(dot(q_ref[:, cols], keys, NT) * (SCALE / score_cap))
        w = jnp.where(mask, jnp.exp2(t * (score_cap * LOG2E)), 0.0)
        part = w[:, :128]
        for c in range(128, w.shape[1], 128):
            part = part + w[:, c : c + 128]
        den[h] += part
        acc[h] += dot(w.astype(jnp.bfloat16), values)

    @pl.when(step == pl.num_programs(0) - 1)
    def _():
        for h in range(heads):
            cols = slice(h * HEAD_DIM, (h + 1) * HEAD_DIM)
            total = jnp.sum(den[h], axis=1, keepdims=True)
            att_ref[:, cols] = (acc[h] / total).astype(jnp.bfloat16)
            lden_ref[h] = jnp.broadcast_to(jnp.log2(total), lden_ref.shape[1:])


def backward_kernel(
    heads, q_ref, qt_ref, g_ref, gt_ref, lden_ref, delta_ref, qpos_ref, k_ref, v_ref, kpos_ref,
    dq_ref, dkv_ref
):
    step = pl.program_id(0)

    @pl.when(step == 0)
    def _():
        dq_ref[...] = jnp.zeros_like(dq_ref)

    keys = k_ref[...]
    values = v_ref[...]
    width = keys.shape[0]
    mask = live(kpos_ref[0], qpos_ref[...])
    dk = jnp.zeros((HEAD_DIM, width), jnp.float32)
    dv = jnp.zeros((HEAD_DIM, width), jnp.float32)
    for h in range(heads):
        cols = slice(h * HEAD_DIM, (h + 1) * HEAD_DIM)
        t = jnp.tanh(dot(q_ref[:, cols], keys, NT) * (SCALE / score_cap))
        p = jnp.exp2(t * (score_cap * LOG2E) - wide(lden_ref[h], width))
        p = jnp.where(mask, p, 0.0)
        dp = dot(g_ref[:, cols], values, NT)
        ds = (p * (dp - wide(delta_ref[h], width)) * (1.0 - t * t)).astype(jnp.bfloat16)
        dv = dv + dot(gt_ref[cols, :], p.astype(jnp.bfloat16))
        dk = dk + dot(qt_ref[cols, :], ds)
        dq_ref[:, cols] += dot(ds, keys)
    rows = dkv_ref.shape[2]
    for b in range(width // rows):
        span = slice(b * rows, (b + 1) * rows)
        dkv_ref[b, :HEAD_DIM, :] = dk[:, span] * SCALE
        dkv_ref[b, HEAD_DIM:, :] = dv[:, span]


def whole(shape):
    return pl.BlockSpec(shape, lambda i: (0,) * len(shape))


PARAMS = pltpu.CompilerParams(
    dimension_semantics=("arbitrary",), vmem_limit_bytes=48 * 1024 * 1024
)


def attention_forward(queries, qpos, keys, values, kpos):
    rows, cols = queries.shape
    heads = cols // HEAD_DIM
    steps = keys.shape[0] // KEY_BLOCK
    block = pl.BlockSpec((KEY_BLOCK, HEAD_DIM), lambda i: (i, 0))
    return pl.pallas_call(
        functools.partial(forward_kernel, heads),
        grid=(steps,),
        in_specs=[
            whole((rows, cols)),
            whole((rows, 128)),
            block,
            block,
            pl.BlockSpec((1, 1, KEY_BLOCK), lambda i: (i, 0, 0)),
        ],
        out_specs=[whole((rows, cols)), whole((heads, rows, 128))],
        out_shape=[
            jax.ShapeDtypeStruct((rows, cols), jnp.bfloat16),
            jax.ShapeDtypeStruct((heads, rows, 128), jnp.float32),
        ],
        scratch_shapes=[
            pltpu.VMEM((heads, rows, HEAD_DIM), jnp.float32),
            pltpu.VMEM((heads, rows, 128), jnp.float32),
        ],
        compiler_params=PARAMS,
        name="attention_forward",
    )(queries, qpos, keys, values, kpos)


def attention_backward(queries, grads, lden, delta, qpos, keys, values, kpos):
    rows, cols = queries.shape
    heads = cols // HEAD_DIM
    steps = keys.shape[0] // KEY_BLOCK
    block = pl.BlockSpec((KEY_BLOCK, HEAD_DIM), lambda i: (i, 0))
    owners = KEY_BLOCK // ROUTED_DEV
    return pl.pallas_call(
        functools.partial(backward_kernel, heads),
        grid=(steps,),
        in_specs=[
            whole((rows, cols)),
            whole((cols, rows)),
            whole((rows, cols)),
            whole((cols, rows)),
            whole((heads, rows, 128)),
            whole((heads, rows, 128)),
            whole((rows, 128)),
            block,
            block,
            pl.BlockSpec((1, 1, KEY_BLOCK), lambda i: (i, 0, 0)),
        ],
        out_specs=[
            whole((rows, cols)),
            pl.BlockSpec((owners, 2 * HEAD_DIM, ROUTED_DEV), lambda i: (i, 0, 0)),
        ],
        out_shape=[
            jax.ShapeDtypeStruct((rows, cols), jnp.float32),
            jax.ShapeDtypeStruct(
                (steps * owners, 2 * HEAD_DIM, ROUTED_DEV), jnp.float32
            ),
        ],
        compiler_params=PARAMS,
        name="attention_backward",
    )(queries, queries.T, grads, grads.T, lden, delta, qpos, keys, values, kpos)


def on_device(
    tokens,
    cotangent,
    norm_gain,
    router_weight,
    w_query,
    w_key,
    w_value,
    w_out,
    routed_index,
    routed_count,
    routed_dest,
):
    seq_devices = lax.axis_size("seq")
    tok_rows, quarter = tokens.shape
    owner_rows = ROUTED_DEV
    pair_slots = 2 * owner_rows // seq_devices
    capacity = routed_index.shape[1]
    local_heads = w_query.shape[1] // HEAD_DIM
    model_width = norm_gain.shape[0]
    buffer_rows = seq_devices * pair_slots
    bf16 = jnp.bfloat16
    listed = jnp.arange(capacity, dtype=jnp.int32)
    is_valid = listed < routed_count[0]
    local_rows = routed_index[0]
    target = routed_dest[0]
    owner_index = jnp.where(is_valid, target // owner_rows, seq_devices)
    place_slot = target % owner_rows
    earlier = jnp.logical_and(
        owner_index[:, None] == owner_index[None, :], listed[None, :] < listed[:, None]
    )
    pair_rank = jnp.sum(earlier.astype(jnp.int32), axis=1)
    buffer_place = jnp.where(is_valid, owner_index * pair_slots + pair_rank, buffer_rows)
    slots = jnp.arange(buffer_rows, dtype=jnp.int32)
    hit = slots[:, None] == buffer_place[None, :]

    def placed(entries, empty):
        found = jnp.sum(jnp.where(hit, entries[None, :] - empty, 0), axis=1)
        return found + empty

    source = placed(local_rows, tok_rows)
    slot_buffer = placed(place_slot, owner_rows)
    pos_buffer = placed(lax.axis_index("seq") * tok_rows + local_rows, 0)
    row_meta = jnp.stack([slot_buffer, pos_buffer], axis=1)
    pick = (source[:, None] == jnp.arange(tok_rows, dtype=jnp.int32)[None, :]).astype(bf16)
    send_x = dot(pick, tokens).astype(bf16)
    send_dy = dot(pick, cotangent).astype(bf16)
    got_meta = lax.all_to_all(row_meta, "seq", split_axis=0, concat_axis=0, tiled=True)
    got_x = lax.all_to_all(send_x, "seq", split_axis=0, concat_axis=0, tiled=True)
    got_dy = lax.all_to_all(send_dy, "seq", split_axis=0, concat_axis=0, tiled=True)
    slot_in = got_meta[:, 0]
    place_hit = jnp.arange(owner_rows, dtype=jnp.int32)[:, None] == slot_in[None, :]
    place = place_hit.astype(bf16)
    compact_x = dot(place, got_x).astype(bf16)
    compact_dy = dot(place, got_dy).astype(bf16)
    row_pos = jnp.sum(jnp.where(place_hit, got_meta[:, 1][None, :], 0), axis=1)
    full_x, full_dy = (
        lax.all_gather(compact_x, "mp", axis=1, tiled=True),
        lax.all_gather(compact_dy, "mp", axis=1, tiled=True),
    )
    x_float = full_x.astype(jnp.float32)
    inv_rms = lax.rsqrt(jnp.mean(x_float * x_float, axis=1) + norm_eps)
    normed = (x_float * inv_rms[:, None] * norm_gain[None, :]).astype(bf16)
    router = jnp.sum(x_float * router_weight[None, :], axis=1)
    queries = dot(normed, w_query).astype(bf16)
    key_rows = dot(normed, w_key).astype(bf16)
    value_rows = dot(normed, w_value).astype(bf16)
    all_keys, all_values, all_pos = (
        lax.all_gather(key_rows, "seq", axis=0, tiled=True),
        lax.all_gather(value_rows, "seq", axis=0, tiled=True),
        lax.all_gather(row_pos, "seq", axis=0, tiled=True),
    )
    kpos = all_pos.reshape(-1, 1, KEY_BLOCK)
    qpos = jnp.broadcast_to(row_pos[:, None], (owner_rows, 128))
    attended, lden = attention_forward(queries, qpos, all_keys, all_values, kpos)
    pulled = dot(full_dy, w_out, NT)
    att_grad = (router[:, None] * pulled).astype(bf16)
    heads_shape = (owner_rows, local_heads, HEAD_DIM)
    att_float = attended.astype(jnp.float32)
    router_part = jnp.sum(pulled * att_float, axis=1)
    row_delta = jnp.sum((att_grad.astype(jnp.float32) * att_float).reshape(heads_shape), axis=2)
    delta = jnp.broadcast_to(row_delta.T[:, :, None], (local_heads, owner_rows, 128))
    query_sum, kv_parts = attention_backward(
        queries, att_grad, lden, delta, qpos, all_keys, all_values, kpos
    )
    kv_grad = lax.psum_scatter(kv_parts, "seq", scatter_dimension=0, tiled=True)[0]
    query_grad = (query_sum * SCALE).astype(bf16)
    key_grad = kv_grad[:HEAD_DIM].astype(bf16)
    value_grad = kv_grad[HEAD_DIM:].astype(bf16)
    summed = dot(w_query, query_grad, NT) + dot(w_key, key_grad) + dot(w_value, value_grad)
    normed_grad = lax.psum_scatter(
        norm_gain[:, None] * summed, "mp", scatter_dimension=0, tiled=True
    )
    x_part = compact_x.astype(jnp.float32).T
    feature_start = lax.axis_index("mp") * quarter
    router_part_w = lax.dynamic_slice_in_dim(router_weight, feature_start, quarter, 0)
    stat_part = jnp.sum(x_part * normed_grad, axis=0)
    router_grad, stat = lax.psum((router_part, stat_part), "mp")
    branch = (
        inv_rms[None, :] * normed_grad
        - x_part * (inv_rms * inv_rms * inv_rms * stat / model_width)[None, :]
        + router_part_w[:, None] * router_grad[None, :]
    ).astype(bf16)
    back_rows = dot(place, branch, (((0,), (1,)), ((), ()))).astype(bf16)
    returned = lax.all_to_all(back_rows, "seq", split_axis=0, concat_axis=0, tiled=True)
    put = (jnp.arange(tok_rows, dtype=jnp.int32)[:, None] == source[None, :]).astype(bf16)
    return (cotangent.astype(jnp.float32) + dot(put, returned)).astype(bf16)


def solution(mesh):
    in_specs = (
        P("seq", "mp"),
        P("seq", "mp"),
        P(),
        P(),
        P(None, "mp"),
        P(None, "mp"),
        P(None, "mp"),
        P("mp", None),
        P("seq", None),
        P("seq"),
        P("seq", None),
    )
    out_specs = P("seq", "mp")
    return jax.shard_map(
        on_device, mesh=mesh, in_specs=in_specs, out_specs=out_specs, check_vma=False
    )
```

time: 632 us -> 458 us (0.72); the launches traced: 622 us -> 457 us
  matrix products: 172 us -> 39.7 us
  Pallas kernels: 0 us -> 57.9 us
  local copies, waits for them, and re-layouts: 57.4 us -> 14.9 us
  other arithmetic: 44.3 us -> 8.7 us
  blocking collectives: 52.3 us -> 80.4 us
  waiting for transfers between devices: 252 us -> 226 us
  starting transfers between devices: 27.8 us -> 15.7 us
    dot_general x120 -> x13, matrix products: 172 us -> 39.7 us  [dot(): return lax.dot_general(a, b, dims, preferred_element_type=jnp.float32)]
    pallas_call x0 -> x2, Pallas kernels: none -> 57.9 us  [the longest x1 36.7 us: attention_backward(): pl.pallas_call(functools.partial(backward_kernel, heads), grid=(steps,),...]
    all_gather x1, waiting for transfers between devices: 45.4 us -> 0.02 us  [on_device(): lax.all_gather(key_rows, 'seq', axis=0, tiled=True)]
    scatter x1 -> x0, other arithmetic: 28.1 us -> none  [on_device(): cotangent.at[jnp.where(is_valid, local_rows, tok_rows)]]
    all_to_all x0 -> x1, blocking collectives: none -> 26.4 us  [on_device(): lax.all_to_all(back_rows, 'seq', split_axis=0, concat_axis=0, tiled=True)]
    all_gather x1, waiting for transfers between devices: 4.27 us -> 28.5 us  [on_device(): lax.all_gather(compact_x, 'mp', axis=1, tiled=True)]
    scatter x7 -> x0, local copies, waits for them, and re-layouts: 19.1 us -> none  [the longest x2 6.91 us: on_device(): jnp.zeros((owner_rows, quarter), jnp.bfloat16).at[slot_in]]
    all_to_all x1 -> x0, waiting for transfers between devices: 16.8 us -> none  [on_device(): lax.all_to_all(back_rows, 'seq', split_axis=1, concat_axis=1, tiled=True)]
  transfers between devices with their start and end apart: 9 -> 8, of which waited for: 7 -> 7; matrix products, arithmetic and copies ran while one was open for 7% -> 5% of each run, Pallas kernels for 0% -> 5%
where the time goes in v1:
time: 458 us; the launch traced here: 457 us
  waiting for transfers between devices  226 us (49%)
  blocking collectives  80.4 us (18%)
  Pallas kernels  57.9 us (13%)
  matrix products  39.7 us (9%)
  starting transfers between devices  15.7 us (3%)
  local copies, waits for them, and re-layouts  14.9 us (3%)
  between operations  14.5 us (3%)
  other arithmetic  8.7 us (2%)
    reduce_scatter x1, waiting for transfers between devices, on_device(): lax.psum_scatter(kv_parts, 'seq', scatter_dimension=0, tiled=True)[0]  91.3 us
    reduce_scatter x1, waiting for transfers between devices, on_device(): lax.psum_scatter(norm_gain[:, None] * summed, 'mp', scatter_dimension=0,...  46.6 us
    dot_general x13, matrix products, dot(): return lax.dot_general(a, b, dims, preferred_element_type=jnp.float32)  39.7 us
    pallas_call x1, Pallas kernels, attention_backward(): pl.pallas_call(functools.partial(backward_kernel, heads), grid=(steps,),...  36.7 us
    all_gather x1, waiting for transfers between devices, on_device(): lax.all_gather(value_rows, 'seq', axis=0, tiled=True)  35.6 us
    all_gather x1, waiting for transfers between devices, on_device(): lax.all_gather(compact_x, 'mp', axis=1, tiled=True)  28.5 us
    all_to_all x1, blocking collectives, on_device(): lax.all_to_all(back_rows, 'seq', split_axis=0, concat_axis=0, tiled=True)  26.4 us
    all_to_all x1, blocking collectives, on_device(): lax.all_to_all(send_dy, 'seq', split_axis=0, concat_axis=0, tiled=True)  24.8 us
  transfers between devices with their start and end apart: 8, of which 7 were waited for; matrix products, arithmetic and copies ran while one was open for 5% of the time, Pallas kernels for 5%

profile of v1, /device:TPU:1, one launch (start us, length us, event | category | flops | bytes accessed | tf_op | source)
XLA Modules:
  0.0 457.4 jit_solution(18388011435382027701)
XLA Ops:
  11.0 9.6 %all-to-all-start = ((s32[32,16,2]{1,2,0:T(2,128)}), s32[32,16,2]{1,2,0:T(2,128)S(1)}, u32[]{:S(2)}, u32[]{:S(2)}) async-start(s32[32,16,2]{1,2,0:T(2,128)} %copy.42), calls=%async_computation | async-start | bytes 65536 | tf_op jit(solution)/shard_map/all_to_all | solution.py:221
  20.6 5.5 %fusion.12 = bf16[512,1024]{1,0:T(8,128)(2,1)} fusion(bf16[2048,1024]{1,0:T(8,128)(2,1)} %param.11, s32[512]{0:T(512)S(1)} %broadcast_add_fusion.2), kind=kOutput, calls=%fused_computation.20 | convolution fusion | flops 2149056512 | bytes 5244928 | tf_op jit(solution)/shard_map/dot_general | solution.py:24
  27.8 5.8 %all-to-all-start.1 = ((bf16[32,16,1024]{2,1,0:T(8,128)(2,1)}), bf16[32,16,1024]{2,1,0:T(8,128)(2,1)S(1)}, u32[]{:S(2)}, u32[]{:S(2)}) async-start(bf16[32,16,1024]{2,1,0:T(8,128)(2,1)} %bitcast.9), calls=%async_computation.1 | async-start | bytes 2097152 | tf_op jit(solution)/shard_map/all_to_all | solution.py:222
  33.8 16.8 %all-to-all-done.1 = bf16[32,16,1024]{2,1,0:T(8,128)(2,1)S(1)} async-done(((bf16[32,16,1024]{2,1,0:T(8,128)(2,1)}), bf16[32,16,1024]{2,1,0:T(8,128)(2,1)S(1)}, u32[]{:S(2)}, u32[]{:S(2)}) %all-to-all-start.1) | async-done | bytes 1048608 | tf_op jit(solution)/shard_map/all_to_all | solution.py:222
  51.9 28.5 %all-gather.6.cloned.1.call-done = bf16[256,4096]{1,0:T(8,128)(2,1)} async-done(((bf16[256,1024]{1,0:T(8,128)(2,1)}), bf16[256,4096]{1,0:T(8,128)(2,1)}) %all-gather.6.cloned.1.call-update) | async-done | bytes 2097168 | tf_op jit(solution)/shard_map/all_gather | solution.py:231
  80.4 3.1 fusion.5
  83.4 3.0 convolution_convert_fusion.5
  86.5 2.7 convolution_convert_fusion.4
  89.3 4.6 fusion.13
  93.8 24.8 %all_to_all.45 = bf16[32,16,1024]{2,1,0:T(8,128)(2,1)S(1)} all-to-all(bf16[32,16,1024]{2,1,0:T(8,128)(2,1)S(1)} %bitcast.69), channel_id=1, replica_groups=mesh['seq'=32,'mp'=4] {'seq'}, dimensions={0} | all-to-all | bytes 2097152 | tf_op jit(solution)/shard_map/all_to_all | solution.py:223
  120.1 22.7 %all-gather = s32[32,1,256]{2,1,0:T(1,128)S(1)} all-gather(s32[1,1,256]{2,1,0:T(1,128)S(1)} %bitcast.75), channel_id=1, replica_groups=mesh['seq'=32,'mp'=4] {'seq'}, dimensions={0}, use_global_device_ids=true | all-gather | bytes 33792 | tf_op jit(solution)/shard_map/all_gather | solution.py:244
  142.8 4.7 %convolution_convert_fusion.3 = bf16[256,512]{0,1:T(8,128)(2,1)S(1)} fusion(bf16[4096,512]{1,0:T(8,128)(2,1)} %param.15, bf16[256,4096]{1,0:T(8,128)(2,1)} %all-gather.6.cloned.1.call-done, f32[256]{0:T(256)S(1)} %add_rsqrt_fusion, f32[4096]{0:T(1024)S(1)} %copy-done.21), kind=kOutput, calls=%fused_computation.25 | convolution fusion | flops 1078067200 | bytes 6571008 | tf_op jit(solution)/shard_map/dot_general | solution.py:24
  147.7 35.6 %all-gather.12.cloned.1.call-done.v_ref = bf16[8192,128]{1,0:T(8,128)(2,1)} async-done(((bf16[256,128]{1,0:T(8,128)(2,1)}), bf16[8192,128]{1,0:T(8,128)(2,1)}) %all-gather.12.cloned.1.call-update) | async-done | bytes 2097168 | tf_op jit(solution)/shard_map/all_gather | solution.py:243
  186.6 21.2 %attention_forward.1 = (bf16[256,512]{1,0:T(8,128)(2,1)S(1)}, f32[4,256,128]{2,1,0:T(8,128)S(1)}) custom-call(bf16[256,512]{1,0:T(8,128)(2,1)S(1)} %copy.48.q_ref, s32[256,128]{1,0:T(8,128)S(1)} %broadcast_in_dim.100.qpos_ref, bf16[8192,128]{1,0:T(8,128)(2,1)S(1)} %copy-done.1, bf16[8192,128]{1,0:T(8,128)(2,1)S(1)} %copy-done.3, s32[16,1,512]{2,1,0:T(1,128)S(1)} %bitcast.63), custom_call_target="tpu_custom_call" | custom-call | tf_op jit(solution)/shard_map/attention_forward/pallas_call | solution.py:114
  209.5 5.0 %all-gather.8.cloned.1.call-done = bf16[256,4096]{1,0:T(8,128)(2,1)} async-done(((bf16[256,1024]{1,0:T(8,128)(2,1)}), bf16[256,4096]{1,0:T(8,128)(2,1)}) %all-gather.8.cloned.1.call-update) | async-done | bytes 2097168 | tf_op jit(solution)/shard_map/all_gather | solution.py:232
  214.5 5.2 %bitcast_reduce_fusion = (f32[256,4]{0,1:T(4,128)S(1)}, bf16[256,512]{0,1:T(8,128)(2,1)}, f32[256,512]{0,1:T(8,128)}) fusion(bf16[256,512]{0,1:T(8,128)(2,1)} %copy.47, f32[256]{0:T(256)} %get-tuple-element.13, bf16[256,4096]{1,0:T(8,128)(2,1)} %all-gather.8.cloned.1.call-done, bf16[512,4096]{1,0:T(8,128)(2,1)} %param.18), kind=kOutput, calls=%fused_computation.44 | convolution fusion | flops 1074527232 | bytes 7345152 | tf_op jit(solution)/shard_map/dot_general | solution.py:24
  226.3 36.7 %attention_backward.1 = (f32[256,512]{1,0:T(8,128)S(1)}, f32[32,256,256]{2,1,0:T(8,128)}) custom-call(bf16[256,512]{1,0:T(8,128)(2,1)S(1)} %copy.48.q_ref, bf16[512,256]{1,0:T(8,128)(2,1)S(1)} %bitcast.61, bf16[256,512]{1,0:T(8,128)(2,1)S(1)} %copy-done.7, bf16[512,256]{1,0:T(8,128)(2,1)S(1)} %bitcast.62, f32[4,256,128]{2,1,0:T(8,128)S(1)} %copy-done.11, ...), custom_call_target="tpu_custom_call" | custom-call | tf_op jit(solution)/shard_map/attention_backward/pallas_call | solution.py:144
  263.9 91.3 %reduce-scatter.3.cloned.1.call-done = f32[1,256,256]{2,1,0:T(8,128)} async-done(((f32[32,256,256]{2,1,0:T(8,128)}), f32[1,256,256]{2,1,0:T(8,128)}) %reduce-scatter.3.cloned.1.call-update) | async-done | bytes 262160 | tf_op jit(solution)/shard_map/reduce_scatter | solution.py:259
  358.8 2.8 fusion.1
  362.8 46.6 %reduce-scatter.5.cloned.1.call-done = f32[1024,256]{0,1:T(8,128)} async-done(((f32[4096,256]{0,1:T(8,128)}), f32[1024,256]{0,1:T(8,128)}) %reduce-scatter.5.cloned.1.call-update) | async-done | bytes 1048592 | tf_op jit(solution)/shard_map/reduce_scatter | solution.py:264
  410.9 6.6 %all-reduce = (f32[256]{0:T(256)S(1)}, f32[256]{0:T(256)S(1)}) all-reduce(f32[256]{0:T(256)S(1)} %fusion.19, f32[256]{0:T(256)S(1)} %fusion.14), channel_id=1, replica_groups=mesh['seq'=32,'mp'=4] {'mp'}, use_global_device_ids=true, to_apply=%region_13.14 | all-reduce | flops 512 | bytes 4096 | tf_op jit(solution)/shard_map/psum | solution.py:271
  417.4 2.1 convolution_convert_fusion
  419.5 26.4 %all_to_all.46 = bf16[32,16,1024]{2,1,0:T(8,128)(2,1)S(1)} all-to-all(bf16[32,16,1024]{2,1,0:T(8,128)(2,1)S(1)} %bitcast.65), channel_id=1, replica_groups=mesh['seq'=32,'mp'=4] {'seq'}, dimensions={0} | all-to-all | bytes 2097152 | tf_op jit(solution)/shard_map/all_to_all | solution.py:278
  445.9 4.6 %add_convert_fusion = bf16[2048,1024]{1,0:T(8,128)(2,1)} fusion(bf16[2048,1024]{1,0:T(8,128)(2,1)S(1)} %copy-done.25, bf16[512,1024]{1,0:T(8,128)(2,1)S(1)} %bitcast.68, s32[512]{0:T(512)S(1)} %copy-done.24), kind=kOutput, calls=%fused_computation | convolution fusion | flops 2154823680 | bytes 9439232 | tf_op jit(solution)/shard_map/dot_general | solution.py:24
  (97 shorter events, 27.1 us)
Async XLA Ops:
  6.5 76.9 %copy-start = (bf16[4096,128]{1,0:T(8,128)(2,1)S(1)}, bf16[4096,128]{1,0:T(8,128)(2,1)}, u32[]{:S(2)}) copy-start(bf16[4096,128]{1,0:T(8,128)(2,1)} %param.16) | copy-start | bytes 3145732
  11.0 16.9 %all-to-all-start = ((s32[32,16,2]{1,2,0:T(2,128)}), s32[32,16,2]{1,2,0:T(2,128)S(1)}, u32[]{:S(2)}, u32[]{:S(2)}) async-start(s32[32,16,2]{1,2,0:T(2,128)} %copy.42), calls=%async_computation | async-start | bytes 65536 | tf_op jit(solution)/shard_map/all_to_all | solution.py:221
  20.6 68.7 %copy-start.23 = (s32[512]{0:T(512)}, s32[512]{0:T(512)S(1)}, u32[]{:S(2)}) copy-start(s32[512]{0:T(512)S(1)} %broadcast_add_fusion.2) | copy-start | bytes 6148
  26.1 54.2 %copy-start.20 = (f32[4096]{0:T(1024)S(1)}, f32[4096]{0:T(1024)}, u32[]{:S(2)}) copy-start(f32[4096]{0:T(1024)} %param.14) | copy-start | bytes 49156
  26.1 57.3 %copy-start.21 = (f32[4096]{0:T(1024)S(1)}, f32[4096]{0:T(1024)}, u32[]{:S(2)}) copy-start(f32[4096]{0:T(1024)} %param.13) | copy-start | bytes 49156
  27.8 22.7 %all-to-all-start.1 = ((bf16[32,16,1024]{2,1,0:T(8,128)(2,1)}), bf16[32,16,1024]{2,1,0:T(8,128)(2,1)S(1)}, u32[]{:S(2)}, u32[]{:S(2)}) async-start(bf16[32,16,1024]{2,1,0:T(8,128)(2,1)} %bitcast.9), calls=%async_computation.1 | async-start | bytes 2097152 | tf_op jit(solution)/shard_map/all_to_all | solution.py:222
  33.7 46.7 %all-gather.6.cloned.1.call-start = ((), (), s32[]{:S(2)}) async-start(), calls=%async_computation.6 | async-start | bytes 2621440 | tf_op jit(solution)/shard_map/all_gather | solution.py:231
  51.8 95.9 %all-gather.10.cloned.1.call-start = ((), (), s32[]{:S(2)}) async-start(), calls=%async_computation.8 | async-start | bytes 2162688 | tf_op jit(solution)/shard_map/all_gather | solution.py:242
  80.4 6.2 %copy-start.16 = (bf16[256,4096]{1,0:T(8,128)(2,1)S(1)}, bf16[256,4096]{1,0:T(8,128)(2,1)}, u32[]{:S(2)}) copy-start(bf16[256,4096]{1,0:T(8,128)(2,1)} %all-gather.6.cloned.1.call-done) | copy-start | bytes 6291460
  86.5 96.9 %all-gather.12.cloned.1.call-start = ((), (), s32[]{:S(2)}) async-start(), calls=%async_computation.9 | async-start | bytes 2162688 | tf_op jit(solution)/shard_map/all_gather | solution.py:243
  89.2 125.3 %all-gather.8.cloned.1.call-start = ((), (), s32[]{:S(2)}) async-start(), calls=%async_computation.7 | async-start | bytes 2621440 | tf_op jit(solution)/shard_map/all_gather | solution.py:232
  119.9 235.3 %reduce-scatter.3.cloned.1.call-start = ((), (), s32[]{:S(2)}) async-start(), calls=%async_computation.10 | async-start | bytes 8650752 | tf_op jit(solution)/shard_map/reduce_scatter | solution.py:259
  142.8 40.7 %copy-start.12 = (s32[32,1,256]{2,1,0:T(1,128)}, s32[32,1,256]{2,1,0:T(1,128)S(1)}, u32[]{:S(2)}) copy-start(s32[32,1,256]{2,1,0:T(1,128)S(1)} %all-gather) | copy-start | bytes 98308
  147.5 67.0 %copy-start.4 = (bf16[256,512]{0,1:T(8,128)(2,1)}, bf16[256,512]{0,1:T(8,128)(2,1)S(1)}, u32[]{:S(2)}) copy-start(bf16[256,512]{0,1:T(8,128)(2,1)S(1)} %convolution_convert_fusion.3) | copy-start | bytes 786436
  183.4 1.6 copy-start.1
  185.0 1.6 copy-start.3
  214.5 7.2 %copy-start.2 = (bf16[8192,128]{1,0:T(8,128)(2,1)S(1)}, bf16[8192,128]{1,0:T(8,128)(2,1)}, u32[]{:S(2)}) copy-start(bf16[8192,128]{1,0:T(8,128)(2,1)} %all-gather.10.cloned.1.call-done.k_ref) | copy-start | bytes 6291460
  263.8 93.3 %copy-start.9 = (f32[256,512]{1,0:T(8,128)S(1)}, f32[256,512]{1,0:T(8,128)}, u32[]{:S(2)}) copy-start(f32[256,512]{1,0:T(8,128)} %copy-done.8) | copy-start | bytes 1572868
  263.8 145.6 %reduce-scatter.5.cloned.1.call-start = ((), (), s32[]{:S(2)}) async-start(), calls=%async_computation.11 | async-start | bytes 5242880 | tf_op jit(solution)/shard_map/reduce_scatter | solution.py:264
  355.2 2.3 copy-start.15
  357.5 1.3 copy-start.22
  361.6 47.9 %copy-start.14 = (bf16[256,1024]{1,0:T(8,128)(2,1)S(1)}, bf16[256,1024]{1,0:T(8,128)(2,1)}, u32[]{:S(2)}) copy-start(bf16[256,1024]{1,0:T(8,128)(2,1)} %convolution_convert_fusion.2) | copy-start | bytes 1572868
  361.6 84.3 %copy-start.24 = (s32[512]{0:T(512)S(1)}, s32[512]{0:T(512)}, u32[]{:S(2)}) copy-start(s32[512]{0:T(512)} %copy-done.23) | copy-start | bytes 6148
  417.4 28.5 %copy-start.25 = (bf16[2048,1024]{1,0:T(8,128)(2,1)S(1)}, bf16[2048,1024]{1,0:T(8,128)(2,1)}, u32[]{:S(2)}) copy-start(bf16[2048,1024]{1,0:T(8,128)(2,1)} %param.12) | copy-start | bytes 12582916
  (10 other events, 9.6 us)
Sparse Core Ops, SparseCore 0:
  51.9 28.3 all-gather.5
  86.6 51.1 all-gather.9
  140.1 43.2 all-gather.11
  184.8 29.5 all-gather.7
  263.9 91.2 reduce-scatter.2
  361.7 47.6 reduce-scatter.4

commit v2 on v1

v2 whole, which is shorter than its diff:
```python
import jax
import jax.numpy as jnp
from jax import lax
from jax.experimental import pallas as pl
from jax.experimental.pallas import tpu as pltpu
from jax.sharding import PartitionSpec as P

HEAD_DIM = 128
ROUTED_DEV = 256
MESH = pl.DeviceIdType.MESH
NT = (((1,), (1,)), ((), ()))
NN = (((1,), (0,)), ((), ()))
TN = (((0,), (0,)), ((), ()))
MIB = 1024 * 1024
norm_eps = 1e-05
score_cap = 5.0
LOG2E = 1.4426950408889634
SCALE = HEAD_DIM ** (-0.5)


def dot(a, b, dims=NN):
    return lax.dot_general(a, b, dims, preferred_element_type=jnp.float32)


def iota(shape, dim):
    return lax.broadcasted_iota(jnp.int32, shape, dim)


def onehot(mask):
    return jnp.where(mask, 1.0, 0.0).astype(jnp.bfloat16)


def remote(src, dst, send_sem, recv_sem, axis, index):
    return pltpu.make_async_remote_copy(
        src_ref=src,
        dst_ref=dst,
        send_sem=send_sem,
        recv_sem=recv_sem,
        device_id={axis: index},
        device_id_type=MESH,
    )


def await_bytes(ref, sem):
    pltpu.make_async_copy(ref, ref, sem).wait()


def greet(axis, count):
    me = lax.axis_index(axis)
    barrier = pltpu.get_barrier_semaphore()

    def body(i, carry):
        pl.semaphore_signal(
            barrier, inc=1, device_id={axis: lax.rem(me + i, count)}, device_id_type=MESH
        )
        return carry

    lax.fori_loop(1, count, body, 0)


def send_pairs(peers, send, got, send_sem, recv_sem, rows):
    me = lax.axis_index("seq")
    mine = pl.ds(pl.multiple_of(me * rows, rows), rows)

    def body(i, carry):
        to = lax.rem(me + i, peers)
        block = send.at[pl.ds(pl.multiple_of(to * rows, rows), rows)]
        remote(block, got.at[mine], send_sem, recv_sem, "seq", to).start()
        return carry

    lax.fori_loop(1, peers, body, 0)
    got[mine, :] = send[mine, :]


def quarter_of(index, width):
    return pl.ds(pl.multiple_of(index * width, width), width)


def ring_send(full, send_sem, recv_sem, stage):
    m = lax.axis_index("mp")
    right, left = lax.rem(m + 1, 4), lax.rem(m + 3, 4)
    half = full.shape[0] // 2
    quarter = full.shape[1] // 4
    top, low = pl.ds(0, half), pl.ds(half, half)

    def move(block, rows, k, to):
        part = full.at[rows, quarter_of(block, quarter)]
        return remote(part, part, send_sem.at[k], recv_sem.at[k], "mp", to)

    if stage == 0:
        copies = [
            move(m, top, 0, right), move(m, low, 1, left),
            move(m, low, 2, right), move(m, top, 3, left),
        ]
        for c in copies:
            c.start()
    elif stage == 1:
        move(left, top, 0, right).wait_recv()
        move(left, top, 4, right).start()
        move(right, low, 1, left).wait_recv()
        move(right, low, 5, left).start()
    else:
        far = lax.rem(m + 2, 4)
        move(left, low, 2, right).wait_recv()
        move(right, top, 3, left).wait_recv()
        move(far, top, 4, right).wait_recv()
        move(far, low, 5, left).wait_recv()
        for k in range(6):
            move(m, top, k, right).wait_send()


def routing_kernel(
    idx_ref, dest_ref, count_ref, tok_hbm, cot_hbm,
    fullx, compactdy, place_ref, source_ref, qpos_ref, kpos_ref,
    tok, cot, pick, sendx, senddy, gotx, gotdy, sendm, gotm,
    load_sem, a2a_send, a2a_recv, mx_send, mx_recv,
):
    peers = lax.axis_size("seq")
    me = lax.axis_index("seq")
    m = lax.axis_index("mp")
    slots = sendx.shape[0]
    tok_rows, quarter = tok.shape
    pair = slots // peers
    load_x = pltpu.make_async_copy(tok_hbm, tok, load_sem.at[0])
    load_d = pltpu.make_async_copy(cot_hbm, cot, load_sem.at[1])
    load_x.start()
    load_d.start()
    greet("seq", peers)
    greet("mp", 4)

    idx = idx_ref[...]
    dest = dest_ref[...]
    listed = iota((1, slots), 1)
    valid = listed < count_ref[0]
    owner = jnp.where(valid, lax.shift_right_logical(dest, 8), peers)
    place_slot = jnp.bitwise_and(dest, ROUTED_DEV - 1)
    rows_i = iota((slots, slots), 0)
    cols_i = iota((slots, slots), 1)
    owner_col = jnp.sum(jnp.where(rows_i == cols_i, owner, 0), axis=1, keepdims=True)
    earlier = jnp.logical_and(owner_col == owner, rows_i < cols_i)
    rank = jnp.sum(jnp.where(earlier, 1, 0), axis=0, keepdims=True)
    buffer_place = jnp.where(valid, owner * pair + rank, slots)
    hit = rows_i == buffer_place
    source = jnp.sum(jnp.where(hit, idx - tok_rows, 0), axis=1, keepdims=True) + tok_rows
    pick[...] = onehot(iota((slots, tok_rows), 1) == source)
    source_row = jnp.sum(
        jnp.where(rows_i == cols_i, source, 0), axis=0, keepdims=True
    )
    source_ref[...] = jnp.broadcast_to(source_row, source_ref.shape)

    owner_hit = iota((peers, slots), 0) == owner
    rank_b = jnp.where(valid, rank, 128)
    lanes = iota((128, slots), 0)

    def spread(entries, shift):
        held = jnp.where(owner_hit, entries, 0).astype(jnp.float32).astype(jnp.bfloat16)
        return dot(held, onehot(lanes == rank_b + shift), NT)

    position = me * tok_rows + idx
    meta = (
        spread(place_slot + 1, 0)
        + spread(lax.shift_right_logical(position, 8), pair)
        + spread(jnp.bitwise_and(position, 255), 2 * pair)
    )
    sendm[...] = jnp.broadcast_to(meta[:, None, :], sendm.shape)

    barrier = pltpu.get_barrier_semaphore()
    pl.semaphore_wait(barrier, peers - 1 + 3)

    def send_meta(i, carry):
        to = lax.rem(me + i, peers)
        remote(
            sendm.at[to], gotm.at[me], a2a_send.at[2], a2a_recv.at[2], "seq", to
        ).start()
        return carry

    lax.fori_loop(1, peers, send_meta, 0)
    gotm[me] = sendm[me]

    def pack(held, send):
        def body(n, carry):
            cols = pl.ds(pl.multiple_of(n * 256, 256), 256)
            send[:, cols] = dot(pick[...], held[:, cols]).astype(jnp.bfloat16)
            return carry

        lax.fori_loop(0, quarter // 256, body, 0)

    load_x.wait()
    pack(tok, sendx)
    send_pairs(peers, sendx, gotx, a2a_send.at[0], a2a_recv.at[0], pair)
    load_d.wait()
    pack(cot, senddy)
    send_pairs(peers, senddy, gotdy, a2a_send.at[1], a2a_recv.at[1], pair)

    others = pl.ds(0, peers - 1)
    await_bytes(gotm.at[others], a2a_recv.at[2])
    got = gotm[:, 0, :].astype(jnp.bfloat16)
    column = iota((128, slots), 0)
    within = jnp.bitwise_and(iota((128, slots), 1), pair - 1)
    sender = iota((peers, slots), 0) == iota((peers, slots), 1) // pair

    def flat(shift):
        spread_out = dot(got, onehot(column == within + shift))
        return jnp.sum(jnp.where(sender, spread_out, 0.0), axis=0, keepdims=True)

    slot_in = flat(0)
    pos_in = flat(pair) * 256.0 + flat(2 * pair)
    here = iota((ROUTED_DEV, slots), 0).astype(jnp.float32) + 1.0 == slot_in
    place_ref[...] = onehot(here)
    qpos = jnp.sum(jnp.where(here, pos_in, 0.0), axis=1, keepdims=True)
    qpos_ref[...] = jnp.broadcast_to(qpos, qpos_ref.shape)
    eye = iota((ROUTED_DEV, ROUTED_DEV), 0) == iota((ROUTED_DEV, ROUTED_DEV), 1)
    kpos = jnp.sum(jnp.where(eye, qpos, 0.0), axis=0, keepdims=True)
    kpos_ref[...] = jnp.broadcast_to(kpos, kpos_ref.shape)

    def compact(got_rows, full, start):
        def body(n, carry):
            cols = pl.ds(pl.multiple_of(n * 256, 256), 256)
            to = pl.ds(pl.multiple_of(start + n * 256, 256), 256)
            full[:, to] = dot(place_ref[...], got_rows[:, cols]).astype(jnp.bfloat16)
            return carry

        lax.fori_loop(0, quarter // 256, body, 0)

    span = pl.ds(0, slots - pair)
    await_bytes(gotx.at[span], a2a_recv.at[0])
    compact(gotx, fullx, m * quarter)
    ring_send(fullx, mx_send, mx_recv, 0)
    await_bytes(gotdy.at[span], a2a_recv.at[1])
    compact(gotdy, compactdy, 0)
    ring_send(fullx, mx_send, mx_recv, 1)
    ring_send(fullx, mx_send, mx_recv, 2)
    await_bytes(sendx.at[span], a2a_send.at[0])
    await_bytes(senddy.at[span], a2a_send.at[1])
    await_bytes(sendm.at[others], a2a_send.at[2])


def route(tokens, cotangent, idx, count, dest):
    peers = lax.axis_size("seq")
    tok_rows, quarter = tokens.shape
    slots = 2 * ROUTED_DEV
    bf16, f32 = jnp.bfloat16, jnp.float32
    vmem = pl.BlockSpec(memory_space=pltpu.VMEM)
    shape = jax.ShapeDtypeStruct
    dma = pltpu.SemaphoreType.DMA
    return pl.pallas_call(
        routing_kernel,
        in_specs=[
            vmem, vmem, pl.BlockSpec(memory_space=pltpu.SMEM),
            pl.BlockSpec(memory_space=pl.ANY), pl.BlockSpec(memory_space=pl.ANY),
        ],
        out_specs=[vmem] * 6,
        out_shape=[
            shape((ROUTED_DEV, 4 * quarter), bf16),
            shape((ROUTED_DEV, quarter), bf16),
            shape((ROUTED_DEV, slots), bf16),
            shape((8, slots), jnp.int32),
            shape((ROUTED_DEV, 128), f32),
            shape((8, ROUTED_DEV), f32),
        ],
        scratch_shapes=[
            pltpu.VMEM((tok_rows, quarter), bf16),
            pltpu.VMEM((tok_rows, quarter), bf16),
            pltpu.VMEM((slots, tok_rows), bf16),
            pltpu.VMEM((slots, quarter), bf16),
            pltpu.VMEM((slots, quarter), bf16),
            pltpu.VMEM((slots, quarter), bf16),
            pltpu.VMEM((slots, quarter), bf16),
            pltpu.VMEM((peers, 8, 128), f32),
            pltpu.VMEM((peers, 8, 128), f32),
            dma((2,)), dma((3,)), dma((3,)), dma((6,)), dma((6,)),
        ],
        compiler_params=pltpu.CompilerParams(
            collective_id=0, has_side_effects=True, vmem_limit_bytes=48 * MIB
        ),
        name="route_rows",
    )(idx, dest, count, tokens, cotangent)


def live(kpos_row, qpos):
    parts = [kpos_row[:, c : c + 128] <= qpos for c in range(0, kpos_row.shape[1], 128)]
    return jnp.concatenate(parts, axis=1)


def wide(column, width):
    return jnp.concatenate([column] * (width // 128), axis=1)


class Place:
    def __init__(self):
        self.me = lax.axis_index("seq")
        self.c = lax.rem(self.me, 2)
        self.sa = 2 + 6 * self.c
        self.sb = 8 - 6 * self.c
        self.a = lax.rem(self.me // self.sa, 4)
        self.b = lax.rem(self.me // self.sb, 4)
        self.sibling = self.me + 1 - 2 * self.c

    def mine(self, i, j):
        return (
            lax.rem(self.a + i, 4) * self.sa + lax.rem(self.b + j, 4) * self.sb + self.c
        )

    def theirs(self, i, j):
        return (
            lax.rem(self.b + i, 4) * self.sb
            + lax.rem(self.a + j, 4) * self.sa
            + 1 - self.c
        )

    def greet(self):
        barrier = pltpu.get_barrier_semaphore()

        def signal(to):
            pl.semaphore_signal(
                barrier, inc=1, device_id={"seq": to}, device_id_type=MESH
            )

        for i in range(1, 4):
            signal(self.mine(i, 0))
            signal(self.mine(0, i))
        signal(self.sibling)
        return 7


def key_block(kv, block):
    rows = kv[block]
    keys = rows[:ROUTED_DEV, :HEAD_DIM]
    values = rows[:ROUTED_DEV, HEAD_DIM:]
    digits = rows[ROUTED_DEV:].astype(jnp.float32)
    return keys, values, digits[0:1] * 256.0 + digits[1:2]


def forward_kernel(
    q_ref, key_ref, value_ref, qpos_ref, kpos_ref, dy_ref,
    att_ref, lden_ref, kv, fulldy,
    acc, den, send_sem, recv_sem, md_send, md_recv,
):
    at = Place()
    heads = acc.shape[0]
    rows = q_ref.shape[0]
    quarter = dy_ref.shape[1]
    waits = at.greet()
    greet("mp", 4)
    kpos = kpos_ref[0:1, :].astype(jnp.int32)
    digits = jnp.where(
        iota((16, rows), 0) == 0,
        lax.shift_right_logical(kpos, 8),
        jnp.bitwise_and(kpos, 255),
    )
    kv[at.me, :rows, :HEAD_DIM] = key_ref[...]
    kv[at.me, :rows, HEAD_DIM:] = value_ref[...]
    kv[at.me, rows:, :] = digits.astype(jnp.float32).astype(jnp.bfloat16)
    fulldy[:, quarter_of(lax.axis_index("mp"), quarter)] = dy_ref[...]
    acc[...] = jnp.zeros_like(acc)
    den[...] = jnp.zeros_like(den)
    pl.semaphore_wait(pltpu.get_barrier_semaphore(), waits + 3)

    def send(block, to):
        here = kv.at[block]
        remote(here, here, send_sem, recv_sem.at[block], "seq", to).start()

    def receive(block):
        await_bytes(kv.at[block], recv_sem.at[block])

    def process(block):
        keys, values, key_pos = key_block(kv, block)
        mask = live(key_pos, qpos_ref[...])
        for h in range(heads):
            cols = slice(h * HEAD_DIM, (h + 1) * HEAD_DIM)
            t = jnp.tanh(dot(q_ref[:, cols], keys, NT) * (SCALE / score_cap))
            w = jnp.where(mask, jnp.exp2(t * (score_cap * LOG2E)), 0.0)
            den[h] += w[:, :128] + w[:, 128:]
            acc[h] += dot(w.astype(jnp.bfloat16), values)

    for i in range(1, 4):
        send(at.me, at.mine(i, 0))
    send(at.me, at.sibling)
    for j in range(1, 4):
        send(at.me, at.mine(0, j))
    ring_send(fulldy, md_send, md_recv, 0)
    process(at.me)

    def order(t):
        late = (t + 12) // 16
        return lax.rem(t, 4), late * (t // 4)

    def step(t, carry):
        block = at.mine(*order(t))
        receive(block)

        @pl.when(t < 4)
        def _():
            for j in range(1, 4):
                send(block, at.mine(0, j))

        send(block, at.sibling)

        @pl.when(t == 6)
        def _():
            ring_send(fulldy, md_send, md_recv, 1)

        other = at.theirs(*order(t - 1))
        receive(other)
        process(other)
        process(block)
        return carry

    lax.fori_loop(1, 16, step, 0)
    last = at.theirs(*order(15))
    receive(last)
    process(last)
    for h in range(heads):
        cols = slice(h * HEAD_DIM, (h + 1) * HEAD_DIM)
        total = jnp.sum(den[h], axis=1, keepdims=True)
        att_ref[:, cols] = (acc[h] / total).astype(jnp.bfloat16)
        lden_ref[h] = jnp.broadcast_to(jnp.log2(total), lden_ref.shape[1:])
    ring_send(fulldy, md_send, md_recv, 2)
    await_bytes(kv.at[pl.ds(0, kv.shape[0] - 1)], send_sem)


def attend(queries, keys, values, qpos, kpos, compact_dy):
    peers = lax.axis_size("seq")
    rows, cols = queries.shape
    heads = cols // HEAD_DIM
    vmem = pl.BlockSpec(memory_space=pltpu.VMEM)
    shape = jax.ShapeDtypeStruct
    dma = pltpu.SemaphoreType.DMA
    return pl.pallas_call(
        forward_kernel,
        in_specs=[vmem] * 6,
        out_specs=[vmem] * 4,
        out_shape=[
            shape((rows, cols), jnp.bfloat16),
            shape((heads, rows, 128), jnp.float32),
            shape((peers, rows + 16, 2 * HEAD_DIM), jnp.bfloat16),
            shape((rows, 4 * compact_dy.shape[1]), jnp.bfloat16),
        ],
        scratch_shapes=[
            pltpu.VMEM((heads, rows, HEAD_DIM), jnp.float32),
            pltpu.VMEM((heads, rows, 128), jnp.float32),
            dma, dma((peers,)), dma((6,)), dma((6,)),
        ],
        compiler_params=pltpu.CompilerParams(
            collective_id=1, has_side_effects=True, vmem_limit_bytes=48 * MIB
        ),
        name="attention_forward",
    )(queries, keys, values, qpos, kpos, compact_dy)


def backward_kernel(
    q_ref, qt_ref, g_ref, gt_ref, lden_ref, delta_ref, qpos_ref, kv,
    dq_ref, dkv_ref,
    dq, to_sib, from_sib, to_b, from_b, to_a, from_a, sends, sib_recv, b_recv, a_recv,
):
    at = Place()
    heads = lden_ref.shape[0]
    waits = at.greet()
    dq[...] = jnp.zeros_like(dq)
    pl.semaphore_wait(pltpu.get_barrier_semaphore(), waits)

    def terms(block):
        keys, values, key_pos = key_block(kv, block)
        width = keys.shape[0]
        mask = live(key_pos, qpos_ref[...])
        dk = jnp.zeros((HEAD_DIM, width), jnp.float32)
        dv = jnp.zeros((HEAD_DIM, width), jnp.float32)
        for h in range(heads):
            cols = slice(h * HEAD_DIM, (h + 1) * HEAD_DIM)
            t = jnp.tanh(dot(q_ref[:, cols], keys, NT) * (SCALE / score_cap))
            p = jnp.exp2(t * (score_cap * LOG2E) - wide(lden_ref[h], width))
            p = jnp.where(mask, p, 0.0)
            dp = dot(g_ref[:, cols], values, NT)
            ds = (p * (dp - wide(delta_ref[h], width)) * (1.0 - t * t)).astype(jnp.bfloat16)
            dv = dv + dot(gt_ref[cols, :], p.astype(jnp.bfloat16))
            dk = dk + dot(qt_ref[cols, :], ds)
            dq[:, cols] += dot(ds, keys)
        return jnp.concatenate([dk * SCALE, dv], axis=0)

    def step(k, carry):
        late = k // 12
        j = (1 + k // 4) * (1 - late)
        i = lax.rem(k + late, 4)
        to_sib[k] = terms(at.theirs(i, j)).astype(jnp.bfloat16)
        remote(
            to_sib.at[k], from_sib.at[k], sends.at[0], sib_recv.at[k], "seq", at.sibling
        ).start()
        own = terms(at.mine(i, j))
        await_bytes(from_sib.at[k], sib_recv.at[k])
        own = own + from_sib[k].astype(jnp.float32)

        @pl.when(late == 0)
        def _():
            to_b[k] = own.astype(jnp.bfloat16)
            slot = (4 - j) * 4 + i
            remote(
                to_b.at[k], from_b.at[slot], sends.at[1], b_recv.at[slot], "seq",
                at.mine(0, j),
            ).start()

        @pl.when(late == 1)
        def _():
            total = own
            for n in range(1, 4):
                await_bytes(from_b.at[n * 4 + i], b_recv.at[n * 4 + i])
                total = total + from_b[n * 4 + i].astype(jnp.float32)

            @pl.when(k < 15)
            def _():
                to_a[i] = total.astype(jnp.bfloat16)
                slot = 4 - i
                remote(
                    to_a.at[i], from_a.at[slot], sends.at[2], a_recv.at[slot], "seq",
                    at.mine(i, 0),
                ).start()

            @pl.when(k == 15)
            def _():
                final = total
                for n in range(1, 4):
                    await_bytes(from_a.at[n], a_recv.at[n])
                    final = final + from_a[n].astype(jnp.float32)
                dkv_ref[...] = final.T.astype(jnp.bfloat16)

        return carry

    lax.fori_loop(0, 16, step, 0)
    dq_ref[...] = (dq[...] * SCALE).astype(jnp.bfloat16)
    await_bytes(to_sib, sends.at[0])
    await_bytes(to_b, sends.at[1])
    await_bytes(to_a.at[pl.ds(0, 3)], sends.at[2])


def attend_backward(queries, grads, lden, delta, qpos, kv):
    rows, cols = queries.shape
    vmem = pl.BlockSpec(memory_space=pltpu.VMEM)
    shape = jax.ShapeDtypeStruct
    dma = pltpu.SemaphoreType.DMA

    def held(n):
        return pltpu.VMEM((n, 2 * HEAD_DIM, rows), jnp.bfloat16)

    return pl.pallas_call(
        backward_kernel,
        in_specs=[vmem] * 8,
        out_specs=[vmem] * 2,
        out_shape=[
            shape((rows, cols), jnp.bfloat16),
            shape((rows, 2 * HEAD_DIM), jnp.bfloat16),
        ],
        scratch_shapes=[
            pltpu.VMEM((rows, cols), jnp.float32),
            held(16), held(16), held(12), held(16), held(4), held(4),
            dma((3,)), dma((16,)), dma((16,)), dma((4,)),
        ],
        compiler_params=pltpu.CompilerParams(
            collective_id=2, has_side_effects=True, vmem_limit_bytes=48 * MIB
        ),
        name="attention_backward",
    )(queries, queries.T, grads, grads.T, lden, delta, qpos, kv)


def as_row(column):
    size = column.shape[0]
    eye = iota((size, size), 0) == iota((size, size), 1)
    return jnp.sum(jnp.where(eye, column, 0.0), axis=0, keepdims=True)


def as_column(row):
    size = row.shape[1]
    eye = iota((size, size), 0) == iota((size, size), 1)
    return jnp.sum(jnp.where(eye, row, 0.0), axis=1, keepdims=True)


def return_kernel(
    dq_ref, dkv_ref, wq_ref, wk_ref, wv_ref, gain_ref, rw_ref, x_ref, inv_ref, part_ref,
    place_ref, got,
    far, near, own, relay, arrived, branch, back, stats, sends, recvs, pair_sems,
):
    peers = lax.axis_size("seq")
    me = lax.axis_index("seq")
    m = lax.axis_index("mp")
    right, left = lax.rem(m + 1, 4), lax.rem(m + 3, 4)
    rows, quarter = x_ref.shape
    half = rows // 2
    slots = got.shape[0]
    pair = slots // peers
    tile = 256
    greet("seq", peers)
    greet("mp", 4)

    def contribution(index, write):
        def body(n, carry):
            f = pl.ds(pl.multiple_of(index * quarter + n * tile, tile), tile)
            cols = pl.ds(pl.multiple_of(n * tile, tile), tile)
            total = dot(dq_ref[...], wq_ref[f, :], NT)
            total = total + dot(dkv_ref[:, :HEAD_DIM], wk_ref[f, :], NT)
            total = total + dot(dkv_ref[:, HEAD_DIM:], wv_ref[f, :], NT)
            write(cols, total * gain_ref[:, f])
            return carry

        lax.fori_loop(0, quarter // tile, body, 0)

    def send(src, dst, k, to):
        copy = remote(src, dst, sends.at[k], recvs.at[k], "mp", to)
        copy.start()
        return copy

    def write_far(cols, total):
        far[:, cols] = total.astype(jnp.bfloat16)

    contribution(lax.rem(m + 2, 4), write_far)
    pl.semaphore_wait(pltpu.get_barrier_semaphore(), peers - 1 + 3)
    top, low = pl.ds(0, half), pl.ds(half, half)
    copies = [
        send(far.at[top], relay.at[0], 0, right),
        send(far.at[low], relay.at[1], 1, left),
    ]

    def write_near(side):
        def write(cols, total):
            near[side, :, cols] = total.astype(jnp.bfloat16)

        return write

    contribution(right, write_near(0))
    copies.append(send(near.at[0, low], arrived.at[0, low], 2, right))
    contribution(left, write_near(1))
    copies.append(send(near.at[1, top], arrived.at[1, top], 3, left))

    def add(side, span):
        summed = near[side, span, :].astype(jnp.float32)
        summed = summed + relay[side].astype(jnp.float32)
        near[side, span, :] = summed.astype(jnp.bfloat16)

    copies[0].wait_recv()
    add(0, slice(0, half))
    copies.append(send(near.at[0, top], arrived.at[0, top], 4, right))
    copies[1].wait_recv()
    add(1, slice(half, rows))
    copies.append(send(near.at[1, low], arrived.at[1, low], 5, left))

    def write_own(cols, total):
        own[:, cols] = total

    contribution(m, write_own)
    for c in copies[2:]:
        c.wait_recv()
    normed_grad = own[...] + arrived[0].astype(jnp.float32) + arrived[1].astype(jnp.float32)
    own[...] = normed_grad
    x = x_ref[...].astype(jnp.float32)
    stat = jnp.sum(x * normed_grad, axis=1, keepdims=True)
    first = iota((8, rows), 0) == 0
    stats[m] = jnp.where(first, as_row(stat), as_row(part_ref[:, 0:1]))

    def send_stats(i, carry):
        to = lax.rem(m + i, 4)
        remote(
            stats.at[m], stats.at[m], pair_sems.at[2], pair_sems.at[3], "mp", to
        ).start()
        return carry

    lax.fori_loop(1, 4, send_stats, 0)
    await_bytes(stats.at[pl.ds(0, 3)], pair_sems.at[3])
    sums = stats[0] + stats[1] + stats[2] + stats[3]
    stat = as_column(sums[0:1])
    router_grad = as_column(sums[1:2])
    inv = inv_ref[:, 0:1]
    factor = inv * inv * inv * stat * (1.0 / (4 * quarter))
    weight = rw_ref[:, quarter_of(m, quarter)]
    branch[...] = (
        inv * own[...] - x * factor + weight * router_grad
    ).astype(jnp.bfloat16)

    def unplace(n, carry):
        cols = pl.ds(pl.multiple_of(n * tile, tile), tile)
        back[:, cols] = dot(place_ref[...], branch[:, cols], TN).astype(jnp.bfloat16)
        return carry

    lax.fori_loop(0, quarter // tile, unplace, 0)
    send_pairs(peers, back, got, pair_sems.at[0], pair_sems.at[1], pair)
    for c in copies:
        c.wait_send()
    await_bytes(stats.at[pl.ds(0, 3)], pair_sems.at[2])
    span = pl.ds(0, slots - pair)
    await_bytes(got.at[span], pair_sems.at[1])
    await_bytes(back.at[span], pair_sems.at[0])


def give_back(dq, dkv, w_query, w_key, w_value, gain, router_weight, x, inv, part, place):
    rows, quarter = x.shape
    slots = place.shape[1]
    vmem = pl.BlockSpec(memory_space=pltpu.VMEM)
    bf16, f32 = jnp.bfloat16, jnp.float32
    dma = pltpu.SemaphoreType.DMA
    return pl.pallas_call(
        return_kernel,
        in_specs=[vmem] * 11,
        out_specs=vmem,
        out_shape=jax.ShapeDtypeStruct((slots, quarter), bf16),
        scratch_shapes=[
            pltpu.VMEM((rows, quarter), bf16),
            pltpu.VMEM((2, rows, quarter), bf16),
            pltpu.VMEM((rows, quarter), f32),
            pltpu.VMEM((2, rows // 2, quarter), bf16),
            pltpu.VMEM((2, rows, quarter), bf16),
            pltpu.VMEM((rows, quarter), bf16),
            pltpu.VMEM((slots, quarter), bf16),
            pltpu.VMEM((4, 8, rows), f32),
            dma((6,)), dma((6,)), dma((4,)),
        ],
        compiler_params=pltpu.CompilerParams(
            collective_id=3, has_side_effects=True, vmem_limit_bytes=48 * MIB
        ),
        name="return_rows",
    )(dq, dkv, w_query, w_key, w_value, gain, router_weight, x, inv, part, place)


def on_device(
    tokens,
    cotangent,
    norm_gain,
    router_weight,
    w_query,
    w_key,
    w_value,
    w_out,
    routed_index,
    routed_count,
    routed_dest,
):
    tok_rows, quarter = tokens.shape
    rows = ROUTED_DEV
    local_heads = w_query.shape[1] // HEAD_DIM
    bf16 = jnp.bfloat16
    full_x, compact_dy, place, source, qpos, kpos = route(
        tokens, cotangent, routed_index, routed_count, routed_dest
    )
    x_float = full_x.astype(jnp.float32)
    inv_rms = lax.rsqrt(jnp.mean(x_float * x_float, axis=1, keepdims=True) + norm_eps)
    normed = (x_float * inv_rms * norm_gain[None, :]).astype(bf16)
    router = jnp.sum(x_float * router_weight[None, :], axis=1)
    queries = dot(normed, w_query).astype(bf16)
    key_rows = dot(normed, w_key).astype(bf16)
    value_rows = dot(normed, w_value).astype(bf16)
    attended, lden, kv, full_dy = attend(
        queries, key_rows, value_rows, qpos, kpos, compact_dy
    )
    pulled = dot(full_dy, w_out, NT)
    att_grad = (router[:, None] * pulled).astype(bf16)
    att_float = attended.astype(jnp.float32)
    router_part = jnp.sum(pulled * att_float, axis=1, keepdims=True)
    products = (att_grad.astype(jnp.float32) * att_float).reshape(rows, local_heads, HEAD_DIM)
    delta = jnp.broadcast_to(
        jnp.sum(products, axis=2).T[:, :, None], (local_heads, rows, 128)
    )
    dq, dkv = attend_backward(queries, att_grad, lden, delta, qpos, kv)
    feature_start = lax.axis_index("mp") * quarter
    x = lax.dynamic_slice_in_dim(full_x, feature_start, quarter, 1)
    returned = give_back(
        dq,
        dkv,
        w_query,
        w_key,
        w_value,
        norm_gain[None, :],
        router_weight[None, :],
        x,
        jnp.broadcast_to(inv_rms, (rows, 128)),
        jnp.broadcast_to(router_part, (rows, 128)),
        place,
    )
    put = (jnp.arange(tok_rows, dtype=jnp.int32)[:, None] == source[0:1]).astype(bf16)
    return (cotangent.astype(jnp.float32) + dot(put, returned)).astype(bf16)


def solution(mesh):
    in_specs = (
        P("seq", "mp"),
        P("seq", "mp"),
        P(),
        P(),
        P(None, "mp"),
        P(None, "mp"),
        P(None, "mp"),
        P("mp", None),
        P("seq", None),
        P("seq"),
        P("seq", None),
    )
    out_specs = P("seq", "mp")
    return jax.shard_map(
        on_device, mesh=mesh, in_specs=in_specs, out_specs=out_specs, check_vma=False
    )
```

time: 458 us -> 217 us (0.47)
  waiting for transfers between devices: 226 us -> 0 us
  Pallas kernels: 57.9 us -> 186 us
  blocking collectives: 80.4 us -> 0 us
  matrix products: 39.7 us -> 13.1 us
  starting transfers between devices: 15.7 us -> 0 us
  between operations: 14.5 us -> 0.93 us
  other arithmetic: 8.7 us -> 1.37 us
    reduce_scatter x2 -> x0, waiting for transfers between devices: 138 us -> none  [the longest x1 91.3 us: on_device(): lax.psum_scatter(kv_parts, 'seq', scatter_dimension=0, tiled=True)[0]]
    pallas_call x2 -> x4, Pallas kernels: 57.9 us -> 186 us  [the longest x1 48.5 us: route(): pl.pallas_call(routing_kernel, in_specs=[vmem, vmem, pl.BlockSpec(memory_...]
    all_gather x4 -> x0, waiting for transfers between devices: 69.1 us -> none  [the longest x1 35.6 us: on_device(): lax.all_gather(value_rows, 'seq', axis=0, tiled=True)]
    all_to_all x2 -> x0, blocking collectives: 51.1 us -> none  [the longest x1 26.4 us: on_device(): lax.all_to_all(back_rows, 'seq', split_axis=0, concat_axis=0, tiled=True)]
    dot_general x13 -> x5, matrix products: 39.7 us -> 13.1 us  [dot(): return lax.dot_general(a, b, dims, preferred_element_type=jnp.float32)]
    all_gather x1 -> x0, blocking collectives: 22.7 us -> none  [on_device(): lax.all_gather(row_pos, 'seq', axis=0, tiled=True)]
    all_to_all x2 -> x0, waiting for transfers between devices: 18.5 us -> none  [the longest x1 16.8 us: on_device(): lax.all_to_all(send_x, 'seq', split_axis=0, concat_axis=0, tiled=True)]
    all_to_all x2 -> x0, starting transfers between devices: 15.4 us -> none  [the longest x1 9.6 us: on_device(): lax.all_to_all(row_meta, 'seq', split_axis=0, concat_axis=0, tiled=True)]
  transfers between devices with their start and end apart: 8 -> 0, of which waited for: 7 -> 0; matrix products, arithmetic and copies ran while one was open for 5% -> 0% of each run, Pallas kernels for 5% -> 0%
where the time goes in v2:
time: 217 us; the launch traced here: 216 us
  Pallas kernels  186 us (86%)
  local copies, waits for them, and re-layouts  14.4 us (7%)
  matrix products  13.1 us (6%)
    pallas_call x1, Pallas kernels, route(): pl.pallas_call(routing_kernel, in_specs=[vmem, vmem, pl.BlockSpec(memory_...  48.5 us
    pallas_call x1, Pallas kernels, attend_backward(): pl.pallas_call(backward_kernel, in_specs=[vmem] * 8, out_specs=[vmem] * 2...  48.1 us
    pallas_call x1, Pallas kernels, attend(): pl.pallas_call(forward_kernel, in_specs=[vmem] * 6, out_specs=[vmem] * 4,...  45.6 us
    pallas_call x1, Pallas kernels, give_back(): pl.pallas_call(return_kernel, in_specs=[vmem] * 11, out_specs=vmem, out_s...  43.6 us
    dot_general x5, matrix products, dot(): return lax.dot_general(a, b, dims, preferred_element_type=jnp.float32)  13.1 us
    unnamed x50, local copies, waits for them, and re-layouts  9.22 us

profile of v2, /device:TPU:1, one launch (start us, length us, event | category | flops | bytes accessed | tf_op | source)
XLA Modules:
  0.0 215.6 jit_solution(10796054287860620120)
XLA Ops:
  0.7 0.7 copy-done.18
  1.3 0.7 copy-done.19
  2.0 48.5 %route_rows.1 = (bf16[256,4096]{1,0:T(8,128)(2,1)S(1)}, bf16[256,1024]{1,0:T(8,128)(2,1)S(1)}, bf16[256,512]{1,0:T(8,128)(2,1)S(1)}, s32[8,512]{1,0:T(8,128)S(1)...) custom-call(s32[1,512]{1,0:T(1,128)S(1)} %copy-done.18, s32[1,512]{1,0:T(1,128)S(1)} %copy-done.19, s32[1]{0:T(128)S(6)} %copy.21.count_ref, ...), custom_call_target="tpu_custom_call" | custom-call | tf_op jit(solution)/shard_map/route_rows/pallas_call | solution.py:246
  51.2 1.3 fusion.3
  52.5 0.9 convolution_convert_fusion.2.key_ref
  53.4 0.9 convolution_convert_fusion.1.value_ref
  54.7 2.0 convolution_convert_fusion
  56.9 1.0 copy-done.7
  58.0 0.7 copy-done.17
  58.7 45.6 %attention_forward.1 = (bf16[256,512]{1,0:T(8,128)(2,1)S(1)}, f32[4,256,128]{2,1,0:T(8,128)S(1)}, bf16[32,272,256]{2,1,0:T(8,128)(2,1)}, bf16[256,4096]{1,0:T(8,128)(2,1)S(1)}) custom-call(bf16[256,512]{1,0:T(8,128)(2,1)S(1)} %copy.16.q_ref, bf16[256,128]{1,0:T(8,128)(2,1)S(1)} %convolution_convert_fusion.2.key_ref, ...), custom_call_target="tpu_custom_call" | custom-call | tf_op jit(solution)/shard_map/attention_forward/pallas_call | solution.py:429
  104.3 0.8 copy-done.4
  105.1 0.7 copy-done.12
  105.8 1.3 copy-done.20
  107.1 1.8 copy.15
  109.0 4.8 %bitcast_reduce_fusion = (f32[256,4]{0,1:T(4,128)}, bf16[256,512]{0,1:T(8,128)(2,1)S(1)}, f32[256,512]{0,1:T(8,128)S(1)}) fusion(bf16[256,512]{0,1:T(8,128)(2,1)} %copy.15, f32[256]{0:T(256)} %get-tuple-element.29, bf16[256,4096]{1,0:T(8,128)(2,1)} %copy-done.20, bf16[512,4096]{1,0:T(8,128)(2,1)} %param.18), kind=kOutput, calls=%fused_computation.17 | convolution fusion | flops 1074527232 | bytes 7345152 | tf_op jit(solution)/shard_map/dot_general | solution.py:22
  113.9 0.8 broadcast_in_dim.14.part_ref
  114.6 0.8 copy.17.g_ref
  115.5 0.9 broadcast_in_dim.10.delta_ref
  116.4 0.9 copy-done.2
  117.4 1.0 copy-done.5
  118.4 0.9 copy-done.9
  119.3 48.1 %attention_backward.1 = (bf16[256,512]{1,0:T(8,128)(2,1)S(1)}, bf16[256,256]{1,0:T(8,128)(2,1)S(1)}) custom-call(bf16[256,512]{1,0:T(8,128)(2,1)S(1)} %copy.16.q_ref, bf16[512,256]{1,0:T(8,128)(2,1)S(1)} %bitcast.14, bf16[256,512]{1,0:T(8,128)(2,1)S(1)} %copy-done.2, bf16[512,256]{1,0:T(8,128)(2,1)S(1)} %bitcast.15, f32[4,256,128]{2,1,0:T(8,128)S(1)} %copy-done.5, ...), custom_call_target="tpu_custom_call" | custom-call | tf_op jit(solution)/shard_map/attention_backward/pallas_call | solution.py:543
  167.5 43.6 %return_rows.1 = bf16[512,1024]{1,0:T(8,128)(2,1)S(1)} custom-call(bf16[256,512]{1,0:T(8,128)(2,1)S(1)} %get-tuple-element.26.dq_ref, bf16[256,256]{1,0:T(8,128)(2,1)S(1)} %get-tuple-element.27.dkv_ref, bf16[4096,512]{1,0:T(8,128)(2,1)} %wq_ref.1, bf16[4096,128]{1,0:T(8,128)(2,1)S(1)} %copy-done, bf16[4096,128]{1,0:T(8,128)(2,1)S(1)} %copy-done.1, ...), custom_call_target="tpu_custom_call" | custom-call | tf_op jit(solution)/shard_map/return_rows/pallas_call | solution.py:696
  211.1 4.5 %add_convert_fusion = bf16[2048,1024]{1,0:T(8,128)(2,1)} fusion(bf16[2048,1024]{1,0:T(8,128)(2,1)S(1)} %copy-done.22, bf16[512,1024]{1,0:T(8,128)(2,1)S(1)} %return_rows.1, s32[512]{0:T(512)S(1)} %bitcast.19), kind=kOutput, calls=%fused_computation | convolution fusion | flops 2154823680 | bytes 9439232 | tf_op jit(solution)/shard_map/dot_general | solution.py:22
  (46 shorter events, 1.4 us)
Async XLA Ops:
  0.7 0.7 copy-start.18
  2.0 49.2 %copy-start.13 = (f32[4096]{0:T(1024)S(1)}, f32[4096]{0:T(1024)}, u32[]{:S(2)}) copy-start(f32[4096]{0:T(1024)} %param.14) | copy-start | bytes 49156
  2.0 50.5 %copy-start = (bf16[4096,128]{1,0:T(8,128)(2,1)S(1)}, bf16[4096,128]{1,0:T(8,128)(2,1)}, u32[]{:S(2)}) copy-start(bf16[4096,128]{1,0:T(8,128)(2,1)} %wk_ref.1) | copy-start | bytes 3145732
  2.0 50.5 %copy-start.14 = (f32[4096]{0:T(1024)S(1)}, f32[4096]{0:T(1024)}, u32[]{:S(2)}) copy-start(f32[4096]{0:T(1024)} %param.13) | copy-start | bytes 49156
  50.6 1.9 copy-start.16
  50.6 3.7 %copy-start.6 = (bf16[256,1024]{1,0:T(8,128)(2,1)}, bf16[256,1024]{1,0:T(8,128)(2,1)S(1)}, u32[]{:S(2)}) copy-start(bf16[256,1024]{1,0:T(8,128)(2,1)S(1)} %get-tuple-element.21.dy_ref) | copy-start | bytes 1572868
  50.6 3.7 %copy-start.10 = (bf16[256,512]{1,0:T(8,128)(2,1)}, bf16[256,512]{1,0:T(8,128)(2,1)S(1)}, u32[]{:S(2)}) copy-start(bf16[256,512]{1,0:T(8,128)(2,1)S(1)} %get-tuple-element.28.place_ref) | copy-start | bytes 786436
  50.6 6.3 %copy-start.8 = (f32[256,128]{1,0:T(8,128)}, f32[256,128]{1,0:T(8,128)S(1)}, u32[]{:S(2)}) copy-start(f32[256,128]{1,0:T(8,128)S(1)} %get-tuple-element.19.qpos_ref) | copy-start | bytes 393220
  50.6 2.8 %copy-start.1 = (bf16[4096,128]{1,0:T(8,128)(2,1)S(1)}, bf16[4096,128]{1,0:T(8,128)(2,1)}, u32[]{:S(2)}) copy-start(bf16[4096,128]{1,0:T(8,128)(2,1)} %wv_ref.1) | copy-start | bytes 3145732
  52.5 2.2 %copy-start.21 = (bf16[4096,512]{1,0:T(8,128)(2,1)S(1)}, bf16[4096,512]{1,0:T(8,128)(2,1)}, u32[]{:S(2)}) copy-start(bf16[4096,512]{1,0:T(8,128)(2,1)} %wq_ref.1) | copy-start | bytes 12582916
  56.9 1.0 copy-start.7
  58.0 0.7 copy-start.17
  104.3 0.8 copy-start.4
  105.1 0.7 copy-start.12
  105.8 1.3 copy-start.20
  108.9 4.8 %copy-start.23 = (bf16[256,512]{0,1:T(8,128)(2,1)S(1)}, bf16[256,512]{0,1:T(8,128)(2,1)}, u32[]{:S(2)}) copy-start(bf16[256,512]{0,1:T(8,128)(2,1)} %copy.15) | copy-start | bytes 786436
  115.5 51.9 %copy-start.3 = (f32[256,128]{1,0:T(8,128)S(1)}, f32[256,128]{1,0:T(8,128)}, u32[]{:S(2)}) copy-start(f32[256,128]{1,0:T(8,128)} %broadcast_in_dim.14.part_ref) | copy-start | bytes 393220
  115.5 51.9 %copy-start.11 = (bf16[256,512]{1,0:T(8,128)(2,1)S(1)}, bf16[256,512]{1,0:T(8,128)(2,1)}, u32[]{:S(2)}) copy-start(bf16[256,512]{1,0:T(8,128)(2,1)} %copy-done.10) | copy-start | bytes 786436
  115.5 51.9 %copy-start.15 = (f32[4096]{0:T(1024)S(1)}, f32[4096]{0:T(1024)}, u32[]{:S(2)}) copy-start(f32[4096]{0:T(1024)} %param.13) | copy-start | bytes 49156
  116.4 1.0 copy-start.2
  117.4 1.0 copy-start.5
  118.4 0.9 copy-start.9
  167.4 43.6 %copy-start.22 = (bf16[2048,1024]{1,0:T(8,128)(2,1)S(1)}, bf16[2048,1024]{1,0:T(8,128)(2,1)}, u32[]{:S(2)}) copy-start(bf16[2048,1024]{1,0:T(8,128)(2,1)} %cot_hbm.1) | copy-start | bytes 12582916
  167.4 43.6 %copy-start.24 = (s32[1,512]{1,0:T(1,128)S(1)}, s32[1,512]{1,0:T(1,128)}, u32[]{:S(2)}) copy-start(s32[1,512]{1,0:T(1,128)} %slice.3) | copy-start | bytes 6148
  (1 other events, 0.7 us)

commit v3 on v0

v3 whole, which is shorter than its diff:
```python
import jax
import jax.numpy as jnp
from jax import lax
from jax.experimental import pallas as pl
from jax.experimental.pallas import tpu as pltpu
from jax.sharding import PartitionSpec as P

HEAD_DIM = 128
ROUTED_DEV = 256
MESH = pl.DeviceIdType.MESH
NT = (((1,), (1,)), ((), ()))
NN = (((1,), (0,)), ((), ()))
TN = (((0,), (0,)), ((), ()))
MIB = 1024 * 1024
VMEM_LIMIT = 60 * MIB
norm_eps = 1e-05
score_cap = 5.0
LOG2E = 1.4426950408889634
SCALE = HEAD_DIM ** (-0.5)


def dot(a, b, dims=NN):
    return lax.dot_general(a, b, dims, preferred_element_type=jnp.float32)


def iota(shape, dim):
    return lax.broadcasted_iota(jnp.int32, shape, dim)


def onehot(mask):
    return jnp.where(mask, 1.0, 0.0).astype(jnp.bfloat16)


def remote(src, dst, send_sem, recv_sem, axis, index):
    return pltpu.make_async_remote_copy(
        src_ref=src,
        dst_ref=dst,
        send_sem=send_sem,
        recv_sem=recv_sem,
        device_id={axis: index},
        device_id_type=MESH,
    )


def await_bytes(ref, sem):
    pltpu.make_async_copy(ref, ref, sem).wait()


def greet(axis, count):
    me = lax.axis_index(axis)
    barrier = pltpu.get_barrier_semaphore()

    def body(i, carry):
        pl.semaphore_signal(
            barrier, inc=1, device_id={axis: lax.rem(me + i, count)}, device_id_type=MESH
        )
        return carry

    lax.fori_loop(1, count, body, 0)


def span_of(start, width):
    return pl.ds(pl.multiple_of(start, width), width)


def send_pairs(peers, send, got, send_sem, recv_sem, rows, cols):
    me = lax.axis_index("seq")
    mine = span_of(me * rows, rows)

    def body(i, carry):
        to = lax.rem(me + i, peers)
        block = send.at[span_of(to * rows, rows), cols]
        remote(block, got.at[mine, cols], send_sem, recv_sem, "seq", to).start()
        return carry

    lax.fori_loop(1, peers, body, 0)
    got[mine, cols] = send[mine, cols]


class Ring:
    def __init__(self, full, send_sem, recv_sem, base, start, width):
        self.full, self.send_sem, self.recv_sem = full, send_sem, recv_sem
        self.base, self.start, self.width = base, start, width
        self.quarter = full.shape[1] // 4
        half = full.shape[0] // 2
        self.top, self.low = pl.ds(0, half), pl.ds(half, half)
        self.m = lax.axis_index("mp")
        self.right, self.left = lax.rem(self.m + 1, 4), lax.rem(self.m + 3, 4)
        self.far = lax.rem(self.m + 2, 4)

    def move(self, block, rows, k, to):
        part = self.full.at[rows, span_of(block * self.quarter + self.start, self.width)]
        k = self.base + k
        return remote(part, part, self.send_sem.at[k], self.recv_sem.at[k], "mp", to)

    def begin(self):
        self.move(self.m, self.top, 0, self.right).start()
        self.move(self.m, self.low, 1, self.left).start()
        self.move(self.m, self.low, 2, self.right).start()
        self.move(self.m, self.top, 3, self.left).start()

    def forward(self):
        self.move(self.left, self.top, 0, self.right).wait_recv()
        self.move(self.left, self.top, 4, self.right).start()
        self.move(self.right, self.low, 1, self.left).wait_recv()
        self.move(self.right, self.low, 5, self.left).start()

    def near(self):
        self.move(self.left, self.low, 2, self.right).wait_recv()
        self.move(self.right, self.top, 3, self.left).wait_recv()

    def end(self):
        self.move(self.far, self.top, 4, self.right).wait_recv()
        self.move(self.far, self.low, 5, self.left).wait_recv()

    def sent(self):
        for k in range(6):
            self.move(self.m, self.top, k, self.right).wait_send()


def live(kpos_row, qpos):
    parts = [kpos_row[:, c : c + 128] <= qpos for c in range(0, kpos_row.shape[1], 128)]
    return jnp.concatenate(parts, axis=1)


def wide(column, width):
    return jnp.concatenate([column] * (width // 128), axis=1)


def lane_parts(x):
    total = x[:, :128]
    for c in range(128, x.shape[1], 128):
        total = total + x[:, c : c + 128]
    return total


def as_row(column):
    size = column.shape[0]
    eye = iota((size, size), 0) == iota((size, size), 1)
    return jnp.sum(jnp.where(eye, column, 0.0), axis=0, keepdims=True)


def as_column(row):
    size = row.shape[1]
    eye = iota((size, size), 0) == iota((size, size), 1)
    return jnp.sum(jnp.where(eye, row, 0.0), axis=1, keepdims=True)


class Place:
    def __init__(self):
        self.me = lax.axis_index("seq")
        self.c = lax.rem(self.me, 2)
        self.sa = 2 + 6 * self.c
        self.sb = 8 - 6 * self.c
        self.a = lax.rem(self.me // self.sa, 4)
        self.b = lax.rem(self.me // self.sb, 4)
        self.sibling = self.me + 1 - 2 * self.c

    def mine(self, i, j):
        return (
            lax.rem(self.a + i, 4) * self.sa + lax.rem(self.b + j, 4) * self.sb + self.c
        )

    def theirs(self, i, j):
        return (
            lax.rem(self.b + i, 4) * self.sb
            + lax.rem(self.a + j, 4) * self.sa
            + 1 - self.c
        )


def key_block(kv, block):
    rows = kv[block]
    keys = rows[:ROUTED_DEV, :HEAD_DIM]
    values = rows[:ROUTED_DEV, HEAD_DIM:]
    digits = rows[ROUTED_DEV:].astype(jnp.float32)
    return keys, values, digits[0:1] * 256.0 + digits[1:2]


CHUNK = 512
TILE = 256


def sublayer_kernel(
    idx_ref, dest_ref, count_ref, gain_ref, rw_ref,
    tok_hbm, cot_hbm, wq_hbm, wk_hbm, wv_hbm, wo_hbm,
    got, source_ref, factor_ref,
    tok, cot, wq, wkv, wo, pick, sendx, senddy, gotx, gotdy, sendm, gotm, sendf, gotf,
    fullx, fulldy, place, qpos, qkv, sums, q4, qt4, g4, gt4, acc, den, lden, delta,
    inv_col, router_col, dq, dqb, dkv,
    kv, to_sib, from_sib, to_b, from_b, to_a, from_a, far, near, relay, arrived, stats,
    load_sem, a2a_send, a2a_recv, x_send, x_recv, d_send, d_recv, kv_send, kv_recv,
    sends, sib_recv, b_recv, a_recv, rs_send, rs_recv, back_send, back_recv, st_send, st_recv,
):
    peers = lax.axis_size("seq")
    m = lax.axis_index("mp")
    at = Place()
    me = at.me
    bf16, f32 = jnp.bfloat16, jnp.float32
    slots = sendx.shape[0]
    tok_rows, quarter = tok.shape
    rows = ROUTED_DEV
    heads = wq.shape[1] // HEAD_DIM
    pair = slots // peers
    right, left, across = lax.rem(m + 1, 4), lax.rem(m + 3, 4), lax.rem(m + 2, 4)
    loads = [
        pltpu.make_async_copy(src, dst, load_sem.at[n])
        for n, (src, dst) in enumerate(
            [
                (tok_hbm, tok),
                (cot_hbm, cot),
                (wq_hbm, wq),
                (wk_hbm, wkv.at[:, pl.ds(0, HEAD_DIM)]),
                (wv_hbm, wkv.at[:, pl.ds(HEAD_DIM, HEAD_DIM)]),
                (wo_hbm, wo),
            ]
        )
    ]
    for load in loads:
        load.start()
    greet("seq", peers)
    greet("mp", 4)

    idx = idx_ref[...]
    dest = dest_ref[...]
    valid = iota((1, slots), 1) < count_ref[0]
    owner = jnp.where(valid, lax.shift_right_logical(dest, 8), peers)
    place_slot = jnp.bitwise_and(dest, rows - 1)
    rows_i = iota((slots, slots), 0)
    cols_i = iota((slots, slots), 1)
    owner_col = jnp.sum(jnp.where(rows_i == cols_i, owner, 0), axis=1, keepdims=True)
    earlier = jnp.logical_and(owner_col == owner, rows_i < cols_i)
    rank = jnp.sum(jnp.where(earlier, 1, 0), axis=0, keepdims=True)
    buffer_place = jnp.where(valid, owner * pair + rank, slots)
    hit = rows_i == buffer_place
    source = jnp.sum(jnp.where(hit, idx - tok_rows, 0), axis=1, keepdims=True) + tok_rows
    pick[...] = onehot(iota((slots, tok_rows), 1) == source)

    lanes = iota((128, slots), 0)

    def spread(hits, entries, lane, shift):
        held = jnp.where(hits, entries, 0.0).astype(bf16)
        return dot(held, onehot(lanes == lane + shift), NT)

    owner_hit = iota((peers, slots), 0) == owner
    rank_lane = jnp.where(valid, rank, 128)
    position = me * tok_rows + idx
    digits = [
        place_slot + 1,
        lax.shift_right_logical(position, 8),
        jnp.bitwise_and(position, 255),
    ]
    meta = sum(
        spread(owner_hit, d.astype(f32), rank_lane, n * pair) for n, d in enumerate(digits)
    )
    sendm[...] = jnp.broadcast_to(meta[:, None, :], sendm.shape)

    pl.semaphore_wait(pltpu.get_barrier_semaphore(), peers - 1 + 3)

    def send_meta(src, dst, k):
        def body(i, carry):
            to = lax.rem(me + i, peers)
            remote(src.at[to], dst.at[me], a2a_send.at[k], a2a_recv.at[k], "seq", to).start()
            return carry

        lax.fori_loop(1, peers, body, 0)
        dst[me] = src[me]

    send_meta(sendm, gotm, 3)

    def pack(held, send, start, width):
        def body(n, carry):
            cols = span_of(start + n * TILE, TILE)
            send[:, cols] = dot(pick[...], held[:, cols]).astype(bf16)
            return carry

        lax.fori_loop(0, width // TILE, body, 0)
        return pl.ds(start, width)

    loads[0].wait()
    for n in range(2):
        cols = pack(tok, sendx, n * CHUNK, CHUNK)
        send_pairs(peers, sendx, gotx, a2a_send.at[n], a2a_recv.at[n], pair, cols)
    loads[1].wait()
    cols = pack(cot, senddy, 0, quarter)
    send_pairs(peers, senddy, gotdy, a2a_send.at[2], a2a_recv.at[2], pair, cols)
    source_row = jnp.sum(jnp.where(rows_i == cols_i, source, 0), axis=0, keepdims=True)
    source_ref[...] = jnp.broadcast_to(source_row, source_ref.shape)

    others = pl.ds(0, peers - 1)
    column = iota((128, slots), 0)
    within = jnp.bitwise_and(iota((128, slots), 1), pair - 1)
    sender = iota((peers, slots), 0) == iota((peers, slots), 1) // pair

    def flat(got_rows, shift):
        out = dot(got_rows, onehot(column == within + shift))
        return jnp.sum(jnp.where(sender, out, 0.0), axis=0, keepdims=True)

    await_bytes(gotm.at[others], a2a_recv.at[3])
    got_meta = gotm[:, 0, :].astype(bf16)
    slot_in = flat(got_meta, 0)
    pos_in = flat(got_meta, pair) * 256.0 + flat(got_meta, 2 * pair)
    here = iota((rows, slots), 0).astype(f32) + 1.0 == slot_in
    place[...] = onehot(here)
    row_pos = jnp.sum(jnp.where(here, pos_in, 0.0), axis=1, keepdims=True)
    qpos[...] = jnp.broadcast_to(row_pos, qpos.shape)
    kpos = as_row(row_pos).astype(jnp.int32)
    pos_digits = jnp.where(
        iota((16, rows), 0) == 0,
        lax.shift_right_logical(kpos, 8),
        jnp.bitwise_and(kpos, 255),
    )
    kv[me, rows:, :] = pos_digits.astype(f32).astype(bf16)

    def compact(got_rows, full, start, width):
        def body(n, carry):
            to = span_of(m * quarter + start + n * TILE, TILE)
            part = got_rows[:, span_of(start + n * TILE, TILE)]
            full[:, to] = dot(place[...], part).astype(bf16)
            return carry

        lax.fori_loop(0, width // TILE, body, 0)

    def arrived_span(ref, width, start=0):
        return ref.at[pl.ds(0, slots - pair), pl.ds(start, width)]

    qkv[...] = jnp.zeros_like(qkv)
    sums[...] = jnp.zeros_like(sums)

    def project(block, start, width):
        f = span_of(block * quarter + start, width)
        x = fullx[:, f].astype(f32)
        sums[0] += lane_parts(x * x)
        sums[1] += lane_parts(x * rw_ref[:, f])
        scaled = (x * gain_ref[:, f]).astype(bf16)
        split = heads * HEAD_DIM
        qkv[:, :split] += dot(scaled, wq[f, :])
        qkv[:, split:] += dot(scaled, wkv[f, :])

    rings = [Ring(fullx, x_send, x_recv, 6 * n, n * CHUNK, CHUNK) for n in range(2)]
    for n in range(2):
        await_bytes(arrived_span(gotx, CHUNK, n * CHUNK), a2a_recv.at[n])
        compact(gotx, fullx, n * CHUNK, CHUNK)
        rings[n].begin()
    for n in range(2, 5):
        loads[n].wait()
    project(m, 0, quarter)
    rings[0].forward()
    rings[0].near()
    project(left, 0, CHUNK)
    project(right, 0, CHUNK)
    rings[1].forward()
    rings[0].end()
    project(across, 0, CHUNK)
    rings[1].near()
    project(left, CHUNK, CHUNK)
    project(right, CHUNK, CHUNK)
    await_bytes(arrived_span(gotdy, quarter), a2a_recv.at[2])
    compact(gotdy, fulldy, 0, quarter)
    rings[1].end()
    project(across, CHUNK, CHUNK)

    mean = jnp.sum(sums[0], axis=1, keepdims=True) * (1.0 / (4 * quarter))
    inv = lax.rsqrt(mean + norm_eps)
    inv_col[...] = jnp.broadcast_to(inv, inv_col.shape)
    router_col[...] = jnp.broadcast_to(
        jnp.sum(sums[1], axis=1, keepdims=True), router_col.shape
    )
    split = heads * HEAD_DIM
    kv[me, :rows, :] = (qkv[:, split:] * inv).astype(bf16)

    half = rows // 2
    whole, top, low = pl.ds(0, rows + 16), pl.ds(0, half), pl.ds(half, half + 16)

    def send(block, to, part=whole):
        span = kv.at[block, part]
        remote(span, span, kv_send, kv_recv.at[block], "seq", to).start()

    def receive(block):
        await_bytes(kv.at[block], kv_recv.at[block])

    send(me, at.mine(1, 0))
    send(me, at.mine(3, 0))
    send(me, at.sibling)
    send(me, at.mine(0, 1))
    send(me, at.mine(0, 3))
    dy_ring = Ring(fulldy, d_send, d_recv, 0, 0, quarter)
    dy_ring.begin()
    for h in range(heads):
        part = (qkv[:, h * HEAD_DIM : (h + 1) * HEAD_DIM] * inv).astype(bf16)
        q4[h * rows : (h + 1) * rows, :] = part
    acc[...] = jnp.zeros_like(acc)
    den[...] = jnp.zeros_like(den)

    def masks(key_pos):
        mask = live(key_pos, qpos[...])
        return jnp.concatenate([mask] * (CHUNK // rows), axis=0)

    def process(block):
        keys, values, key_pos = key_block(kv, block)
        mask = masks(key_pos)
        for start in range(0, heads * rows, CHUNK):
            r = slice(start, start + CHUNK)
            t = jnp.tanh(dot(q4[r, :], keys, NT) * (SCALE / score_cap))
            w = jnp.where(mask, jnp.exp2(t * (score_cap * LOG2E)), 0.0)
            den[r] += lane_parts(w)
            acc[r] += dot(w.astype(bf16), values)

    def order(t):
        a = (t + 12) // 16
        b = (t + 4) // 16
        u = (1 - a) * t + (a - b) * lax.div(t - 4, 2) + b * (t - 12)
        i = u + (u // 2) * (1 - 2 * lax.rem(u, 2))
        j = (a - b) * (1 + 2 * lax.rem(t, 2)) + 2 * b
        return i, j

    def take(t):
        block = at.mine(*order(t))
        receive(block)

        @pl.when(t == 1)
        def _():
            send(block, at.mine(3, 0), low)

        @pl.when(t == 2)
        def _():
            send(block, at.mine(1, 0), top)

        @pl.when(t < 4)
        def _():
            send(block, at.mine(0, 1))
            send(block, at.mine(0, 3))

        @pl.when(jnp.logical_and(t >= 4, t < 12))
        def _():
            @pl.when(lax.rem(t, 2) == 0)
            def _():
                send(block, at.mine(0, 3), low)

            @pl.when(lax.rem(t, 2) == 1)
            def _():
                send(block, at.mine(0, 1), top)

        send(block, at.sibling)
        return block

    def pair_of(t):
        a, b = at.theirs(*order(t)), at.theirs(*order(t + 1))
        receive(a)
        receive(b)
        return a, b

    process(me)
    for h in range(heads):
        r = slice(h * rows, (h + 1) * rows)
        qt4[:, r] = q4[r, :].T

    def step(s, carry):
        t = 1 + 2 * s
        a = take(t)
        b = take(t + 1)

        @pl.when(s == 2)
        def _():
            dy_ring.forward()

        process(a)
        process(b)
        c, d = pair_of(t - 1)
        process(c)
        process(d)
        return carry

    lax.fori_loop(0, 7, step, 0)
    a = take(15)
    process(a)
    c, d = pair_of(14)
    process(c)
    process(d)

    loads[5].wait()
    dy_ring.near()
    dy_ring.end()
    router = router_col[...]
    dots = jnp.zeros((rows, 1), f32)
    for n in range(split // TILE):
        pulled = dot(fulldy[...], wo[n * TILE : (n + 1) * TILE, :], NT)
        for g in range(TILE // HEAD_DIM):
            h = n * (TILE // HEAD_DIM) + g
            r = slice(h * rows, (h + 1) * rows)
            mine = pulled[:, g * HEAD_DIM : (g + 1) * HEAD_DIM]
            total = jnp.sum(den[r], axis=1, keepdims=True)
            att = (acc[r] / total).astype(bf16).astype(f32)
            lden[r] = jnp.broadcast_to(jnp.log2(total), (rows, 128))
            grad = (mine * router).astype(bf16)
            g4[r, :] = grad
            gt4[:, r] = grad.T
            row_delta = jnp.sum(grad.astype(f32) * att, axis=1, keepdims=True)
            delta[r] = jnp.broadcast_to(row_delta, (rows, 128))
            dots = dots + jnp.sum(mine * att, axis=1, keepdims=True)

    def send_stats(k):
        def body(i, carry):
            to = lax.rem(m + i, 4)
            here = stats.at[k, m]
            remote(here, here, st_send.at[k], st_recv.at[k], "mp", to).start()
            return carry

        lax.fori_loop(1, 4, body, 0)

    def take_stats(k):
        await_bytes(stats.at[k, pl.ds(0, 3)], st_recv.at[k])
        return as_column((stats[k, 0] + stats[k, 1] + stats[k, 2] + stats[k, 3])[0:1])

    stats[0, m] = jnp.broadcast_to(as_row(dots), stats.shape[2:])
    send_stats(0)

    dq[...] = jnp.zeros_like(dq)

    def terms(block):
        keys, values, key_pos = key_block(kv, block)
        width = keys.shape[0]
        mask = masks(key_pos)
        probs, grads = [], []
        for start in range(0, heads * rows, CHUNK):
            r = slice(start, start + CHUNK)
            t = jnp.tanh(dot(q4[r, :], keys, NT) * (SCALE / score_cap))
            p = jnp.exp2(t * (score_cap * LOG2E) - wide(lden[r], width))
            p = jnp.where(mask, p, 0.0)
            dp = dot(g4[r, :], values, NT)
            probs.append(p.astype(bf16))
            grads.append((p * (dp - wide(delta[r], width)) * (1.0 - t * t)).astype(bf16))
        probs, grads = jnp.concatenate(probs, axis=0), jnp.concatenate(grads, axis=0)
        dq[...] += dot(grads, keys)
        dk = dot(qt4[...], grads) * SCALE
        return jnp.concatenate([dk, dot(gt4[...], probs)], axis=0)

    def pass_on(k, late, i, j):
        await_bytes(from_sib.at[k], sib_recv.at[k])

        @pl.when(late == 0)
        def _():
            summed = to_b[k].astype(f32) + from_sib[k].astype(f32)
            to_b[k] = summed.astype(bf16)
            slot = (4 - j) * 4 + i
            remote(
                to_b.at[k], from_b.at[slot], sends.at[1], b_recv.at[slot], "seq",
                at.mine(0, j),
            ).start()

        @pl.when(late == 1)
        def _():
            total = to_b[k].astype(f32) + from_sib[k].astype(f32)
            for n in range(1, 4):
                await_bytes(from_b.at[n * 4 + i], b_recv.at[n * 4 + i])
                total = total + from_b[n * 4 + i].astype(f32)

            @pl.when(k < 15)
            def _():
                to_a[i] = total.astype(bf16)
                slot = 4 - i
                remote(
                    to_a.at[i], from_a.at[slot], sends.at[2], a_recv.at[slot], "seq",
                    at.mine(i, 0),
                ).start()

            @pl.when(k == 15)
            def _():
                final = total
                for n in range(1, 4):
                    await_bytes(from_a.at[n], a_recv.at[n])
                    final = final + from_a[n].astype(f32)
                dkv[...] = final.T.astype(bf16)

    def back_step(s, carry):
        late = s // 6
        places = []
        for n in range(2):
            k = 2 * s + n
            j = (1 + k // 4) * (1 - late)
            i = lax.rem(k + late, 4)
            places.append((k, late, i, j))
        for k, _, i, j in places:
            to_sib[k] = terms(at.theirs(i, j)).astype(bf16)
            remote(
                to_sib.at[k], from_sib.at[k], sends.at[0], sib_recv.at[k], "seq", at.sibling
            ).start()
        for k, _, i, j in places:
            to_b[k] = terms(at.mine(i, j)).astype(bf16)
        for where in places:
            pass_on(*where)
        return carry

    lax.fori_loop(0, 8, back_step, 0)
    for h in range(heads):
        r = slice(h * rows, (h + 1) * rows)
        dqb[:, h * HEAD_DIM : (h + 1) * HEAD_DIM] = (dq[r] * SCALE).astype(bf16)

    chunks = quarter // TILE

    def contribution(block, n):
        f = span_of(block * quarter + n * TILE, TILE)
        total = dot(dqb[...], wq[f, :], NT) + dot(dkv[...], wkv[f, :], NT)
        return total * gain_ref[:, f]

    def rs(src, dst, n, k, to):
        k = 6 * n + k
        return remote(src, dst, rs_send.at[k], rs_recv.at[k], "mp", to)

    top, low = pl.ds(0, half), pl.ds(half, half)
    copies = []

    def hand_over(n):
        cols = pl.ds(n * TILE, TILE)
        copies[n][0].wait_recv()
        near[0, top, cols] = (
            near[0, top, cols].astype(f32) + relay[0, :, cols].astype(f32)
        ).astype(bf16)
        copies[n].append(rs(near.at[0, top, cols], arrived.at[0, top, cols], n, 4, right))
        copies[n][4].start()
        copies[n][1].wait_recv()
        near[1, low, cols] = (
            near[1, low, cols].astype(f32) + relay[1, :, cols].astype(f32)
        ).astype(bf16)
        copies[n].append(rs(near.at[1, low, cols], arrived.at[1, low, cols], n, 5, left))
        copies[n][5].start()

    for n in range(chunks):
        cols = pl.ds(n * TILE, TILE)
        far[:, cols] = contribution(across, n).astype(bf16)
        first = rs(far.at[top, cols], relay.at[0, :, cols], n, 0, right)
        second = rs(far.at[low, cols], relay.at[1, :, cols], n, 1, left)
        first.start()
        second.start()
        near[0, :, cols] = contribution(right, n).astype(bf16)
        third = rs(near.at[0, low, cols], arrived.at[0, low, cols], n, 2, right)
        third.start()
        near[1, :, cols] = contribution(left, n).astype(bf16)
        fourth = rs(near.at[1, top, cols], arrived.at[1, top, cols], n, 3, left)
        fourth.start()
        copies.append([first, second, third, fourth])
        if n > 0:
            hand_over(n - 1)
    hand_over(chunks - 1)

    router_grad = take_stats(0)
    await_bytes(arrived_span(sendx, CHUNK), a2a_send.at[0])
    await_bytes(arrived_span(sendx, CHUNK, CHUNK), a2a_send.at[1])
    back = sendx
    inv = inv_col[:, 0:1]
    stat = jnp.zeros((rows, 128), f32)
    for n in range(chunks):
        cols = pl.ds(n * TILE, TILE)
        f = span_of(m * quarter + n * TILE, TILE)
        own = contribution(m, n)
        for c in copies[n][2:]:
            c.wait_recv()
        own = own + arrived[0, :, cols].astype(f32) + arrived[1, :, cols].astype(f32)
        stat = stat + lane_parts(fullx[:, f].astype(f32) * own)
        branch = (inv * own + rw_ref[:, f] * router_grad).astype(bf16)
        back[:, cols] = dot(place[...], branch, TN).astype(bf16)
        send_pairs(peers, back, got, back_send.at[n], back_recv.at[n], pair, cols)

    stats[1, m] = jnp.broadcast_to(
        as_row(jnp.sum(stat, axis=1, keepdims=True)), stats.shape[2:]
    )
    send_stats(1)
    factor = inv * inv * inv * take_stats(1) * (1.0 / (4 * quarter))
    rest = jnp.sum(jnp.where(place[...].astype(f32) > 0.5, factor, 0.0), axis=0, keepdims=True)
    slot_lane = jnp.bitwise_and(iota((1, slots), 1), pair - 1)
    meta = jnp.zeros((peers, 128), f32)
    for n in range(3):
        piece = rest.astype(bf16).astype(f32)
        rest = rest - piece
        meta = meta + spread(sender, piece, slot_lane, n * pair)
    sendf[...] = jnp.broadcast_to(meta[:, None, :], sendf.shape)
    send_meta(sendf, gotf, 4)
    await_bytes(gotf.at[others], a2a_recv.at[4])
    got_meta = gotf[:, 0, :].astype(bf16)
    factor_row = flat(got_meta, 0) + flat(got_meta, pair) + flat(got_meta, 2 * pair)
    factor_ref[...] = jnp.broadcast_to(factor_row, factor_ref.shape)

    for n in range(chunks):
        await_bytes(arrived_span(got, TILE, n * TILE), back_recv.at[n])
        await_bytes(arrived_span(back, TILE, n * TILE), back_send.at[n])
    await_bytes(arrived_span(senddy, quarter), a2a_send.at[2])
    await_bytes(sendm.at[others], a2a_send.at[3])
    await_bytes(sendf.at[others], a2a_send.at[4])
    for ring in rings:
        ring.sent()
    dy_ring.sent()
    for group in copies:
        for c in group:
            c.wait_send()
    for k in range(2):
        await_bytes(stats.at[k, pl.ds(0, 3)], st_send.at[k])
    await_bytes(to_sib, sends.at[0])
    await_bytes(to_b.at[pl.ds(0, 12)], sends.at[1])
    await_bytes(to_a.at[pl.ds(0, 3)], sends.at[2])
    await_bytes(kv.at[others], kv_send)


def sublayer(tokens, cotangent, gain, router_weight, w_query, w_key, w_value, w_out, idx, count, dest):
    peers = lax.axis_size("seq")
    tok_rows, quarter = tokens.shape
    width = 4 * quarter
    split = w_query.shape[1]
    heads = split // HEAD_DIM
    rows = ROUTED_DEV
    slots = 2 * rows
    bf16, f32 = jnp.bfloat16, jnp.float32
    vmem = pl.BlockSpec(memory_space=pltpu.VMEM)
    hbm = pl.BlockSpec(memory_space=pl.ANY)
    shape = jax.ShapeDtypeStruct
    dma = pltpu.SemaphoreType.DMA
    ram = pltpu.VMEM
    stacked = heads * rows

    def held(n):
        return ram((n, 2 * HEAD_DIM, rows), bf16)

    return pl.pallas_call(
        sublayer_kernel,
        in_specs=[vmem, vmem, pl.BlockSpec(memory_space=pltpu.SMEM), vmem, vmem] + [hbm] * 6,
        out_specs=[vmem] * 3,
        out_shape=[
            shape((slots, quarter), bf16),
            shape((8, slots), jnp.int32),
            shape((8, slots), f32),
        ],
        scratch_shapes=[
            ram((tok_rows, quarter), bf16), ram((tok_rows, quarter), bf16),
            ram((width, split), bf16), ram((width, 2 * HEAD_DIM), bf16), ram((split, width), bf16),
            ram((slots, tok_rows), bf16),
            ram((slots, quarter), bf16), ram((slots, quarter), bf16),
            ram((slots, quarter), bf16), ram((slots, quarter), bf16),
            ram((peers, 8, 128), f32), ram((peers, 8, 128), f32),
            ram((peers, 8, 128), f32), ram((peers, 8, 128), f32),
            ram((rows, width), bf16), ram((rows, width), bf16),
            ram((rows, slots), bf16), ram((rows, 128), f32),
            ram((rows, split + 2 * HEAD_DIM), f32), ram((2, rows, 128), f32),
            ram((stacked, HEAD_DIM), bf16), ram((HEAD_DIM, stacked), bf16),
            ram((stacked, HEAD_DIM), bf16), ram((HEAD_DIM, stacked), bf16),
            ram((stacked, HEAD_DIM), f32), ram((stacked, 128), f32),
            ram((stacked, 128), f32), ram((stacked, 128), f32),
            ram((rows, 128), f32), ram((rows, 128), f32),
            ram((stacked, HEAD_DIM), f32), ram((rows, split), bf16),
            ram((rows, 2 * HEAD_DIM), bf16),
            ram((peers, rows + 16, 2 * HEAD_DIM), bf16),
            held(16), held(16), held(16), held(16), held(4), held(4),
            ram((rows, quarter), bf16), ram((2, rows, quarter), bf16),
            ram((2, rows // 2, quarter), bf16), ram((2, rows, quarter), bf16),
            ram((2, 4, 8, rows), f32),
            dma((6,)), dma((5,)), dma((5,)), dma((12,)), dma((12,)), dma((6,)), dma((6,)),
            dma, dma((peers,)),
            dma((3,)), dma((16,)), dma((16,)), dma((4,)), dma((24,)), dma((24,)),
            dma((4,)), dma((4,)), dma((2,)), dma((2,)),
        ],
        compiler_params=pltpu.CompilerParams(
            collective_id=0, has_side_effects=True, vmem_limit_bytes=VMEM_LIMIT
        ),
        name="sublayer",
    )(
        idx, dest, count, gain, router_weight,
        tokens, cotangent, w_query, w_key, w_value, w_out,
    )


def final_kernel(tok_ref, cot_ref, got_ref, source_ref, factor_ref, out_ref):
    block, slots = tok_ref.shape[0], got_ref.shape[0]
    first = pl.program_id(0) * block
    put = iota((block, slots), 0) + first == source_ref[0:1, :]
    factor = jnp.sum(jnp.where(put, factor_ref[0:1, :], 0.0), axis=1, keepdims=True)
    moved = dot(onehot(put), got_ref[...])
    out = cot_ref[...].astype(jnp.float32) + moved
    out_ref[...] = (out - tok_ref[...].astype(jnp.float32) * factor).astype(jnp.bfloat16)


def finish(tokens, cotangent, got, source, factor):
    tok_rows, quarter = tokens.shape
    block = pl.BlockSpec((256, quarter), lambda i: (i, 0))

    def whole(array):
        return pl.BlockSpec(array.shape, lambda i: (0, 0))

    return pl.pallas_call(
        final_kernel,
        grid=(tok_rows // 256,),
        in_specs=[block, block, whole(got), whole(source), whole(factor)],
        out_specs=block,
        out_shape=jax.ShapeDtypeStruct(tokens.shape, jnp.bfloat16),
        compiler_params=pltpu.CompilerParams(
            dimension_semantics=("arbitrary",), vmem_limit_bytes=32 * MIB
        ),
        name="add_branch",
    )(tokens, cotangent, got, source, factor)


def on_device(
    tokens,
    cotangent,
    norm_gain,
    router_weight,
    w_query,
    w_key,
    w_value,
    w_out,
    routed_index,
    routed_count,
    routed_dest,
):
    got, source, factor = sublayer(
        tokens,
        cotangent,
        norm_gain[None, :],
        router_weight[None, :],
        w_query,
        w_key,
        w_value,
        w_out,
        routed_index,
        routed_count,
        routed_dest,
    )
    return finish(tokens, cotangent, got, source, factor)


def solution(mesh):
    in_specs = (
        P("seq", "mp"),
        P("seq", "mp"),
        P(),
        P(),
        P(None, "mp"),
        P(None, "mp"),
        P(None, "mp"),
        P("mp", None),
        P("seq", None),
        P("seq"),
        P("seq", None),
    )
    out_specs = P("seq", "mp")
    return jax.shard_map(
        on_device, mesh=mesh, in_specs=in_specs, out_specs=out_specs, check_vma=False
    )
```

time: 632 us -> 157 us (0.25); the launches traced: 622 us -> 157 us
  waiting for transfers between devices: 252 us -> 0 us
  matrix products: 172 us -> 0 us
  Pallas kernels: 0 us -> 149 us
  blocking collectives: 52.3 us -> 0 us
  local copies, waits for them, and re-layouts: 57.4 us -> 7.03 us
  other arithmetic: 44.3 us -> 0 us
  starting transfers between devices: 27.8 us -> 0 us
  between operations: 15 us -> 0.67 us
    dot_general x120 -> x0, matrix products: 172 us -> none  [the longest x16 31.2 us: score_grads(): jnp.einsum('rgd,kd->rgk', grad_heads, value_rows, preferred_element_type=...]
    pallas_call x0 -> x2, Pallas kernels: none -> 149 us  [the longest x1 143 us: sublayer(): pl.pallas_call(sublayer_kernel, in_specs=[vmem, vmem, pl.BlockSpec(memory...]
    reduce_scatter x2 -> x0, waiting for transfers between devices: 133 us -> none  [the longest x1 89.8 us: on_device(): lax.psum_scatter(kv_parts.reshape(key_count, 2 * head_dim), 'seq', scatte...]
    all_gather x4 -> x0, waiting for transfers between devices: 85.9 us -> none  [the longest x1 45.4 us: on_device(): lax.all_gather(key_rows, 'seq', axis=0, tiled=True)]
    all_to_all x3 -> x0, waiting for transfers between devices: 33.1 us -> none  [the longest x1 16.8 us: on_device(): lax.all_to_all(back_rows, 'seq', split_axis=1, concat_axis=1, tiled=True)]
    scatter x1 -> x0, other arithmetic: 28.1 us -> none  [on_device(): cotangent.at[jnp.where(is_valid, local_rows, tok_rows)]]
    all_to_all x3 -> x0, starting transfers between devices: 27.1 us -> none  [the longest x1 10 us: on_device(): lax.all_to_all(back_rows, 'seq', split_axis=1, concat_axis=1, tiled=True)]
    all_gather x1 -> x0, blocking collectives: 25 us -> none  [on_device(): lax.all_gather(row_pos, 'seq', axis=0, tiled=True)]
  transfers between devices with their start and end apart: 9 -> 0, of which waited for: 7 -> 0; matrix products, arithmetic and copies ran while one was open for 7% -> 0% of each run, Pallas kernels for 0% -> 0%
where the time goes in v3:
time: 157 us
  Pallas kernels  149 us (95%)
  local copies, waits for them, and re-layouts  7.03 us (4%)
    pallas_call x1, Pallas kernels, sublayer(): pl.pallas_call(sublayer_kernel, in_specs=[vmem, vmem, pl.BlockSpec(memory...  143 us
    unnamed x10, local copies, waits for them, and re-layouts  7.03 us
    pallas_call x1, Pallas kernels, finish(): pl.pallas_call(final_kernel, grid=(tok_rows // 256,), in_specs=[block, bl...  5.53 us

profile of v3, /device:TPU:1, one launch (start us, length us, event | category | flops | bytes accessed | tf_op | source)
XLA Modules:
  0.0 156.7 jit_solution(2496058795079453933)
XLA Ops:
  0.7 143.5 %sublayer.1 = (bf16[512,1024]{1,0:T(8,128)(2,1)}, s32[8,512]{1,0:T(8,128)}, f32[8,512]{1,0:T(8,128)}) custom-call(s32[1,512]{1,0:T(1,128)} %idx_ref.1, s32[1,512]{1,0:T(1,128)} %dest_ref.1, s32[1]{0:T(128)S(6)} %copy.12.count_ref, f32[1,4096]{1,0:T(1,128)} %bitcast.2, f32[1,4096]{1,0:T(1,128)} %bitcast.3, bf16[2048,1024]{1,0:T(8,128)(2,1)} %tok_ref.1, ...), custom_call_target="tpu_custom_call" | custom-call | tf_op jit(solution)/shard_map/sublayer/pallas_call | solution.py:722
  144.1 0.0 copy-start
  144.1 2.2 %copy-done = bf16[2048,1024]{1,0:T(8,128)(2,1)S(1)} copy-done((bf16[2048,1024]{1,0:T(8,128)(2,1)S(1)}, bf16[2048,1024]{1,0:T(8,128)(2,1)}, u32[]{:S(2)}) %copy-start) | copy-done | bytes 4194328
  146.3 0.0 copy-start.1
  146.3 2.2 %copy-done.1 = bf16[2048,1024]{1,0:T(8,128)(2,1)S(1)} copy-done((bf16[2048,1024]{1,0:T(8,128)(2,1)S(1)}, bf16[2048,1024]{1,0:T(8,128)(2,1)}, u32[]{:S(2)}) %copy-start.1) | copy-done | bytes 4194328
  148.5 0.0 copy-start.2
  148.5 1.2 copy-done.2
  149.7 0.0 copy-start.3
  149.7 0.7 copy-done.3
  150.4 0.0 copy-start.4
  150.4 0.7 copy-done.4
  151.2 5.5 %add_branch.1 = bf16[2048,1024]{1,0:T(8,128)(2,1)} custom-call(bf16[2048,1024]{1,0:T(8,128)(2,1)S(1)} %copy-done, bf16[2048,1024]{1,0:T(8,128)(2,1)S(1)} %copy-done.1, bf16[512,1024]{1,0:T(8,128)(2,1)S(1)} %copy-done.2, s32[8,512]{1,0:T(8,128)S(1)} %copy-done.3, f32[8,512]{1,0:T(8,128)S(1)} %copy-done.4), custom_call_target="tpu_custom_call" | custom-call | tf_op jit(solution)/shard_map/add_branch/pallas_call | solution.py:786
Async XLA Ops:
  144.1 2.2 %copy-start = (bf16[2048,1024]{1,0:T(8,128)(2,1)S(1)}, bf16[2048,1024]{1,0:T(8,128)(2,1)}, u32[]{:S(2)}) copy-start(bf16[2048,1024]{1,0:T(8,128)(2,1)} %tok_ref.1) | copy-start | bytes 12582916
  146.3 2.2 %copy-start.1 = (bf16[2048,1024]{1,0:T(8,128)(2,1)S(1)}, bf16[2048,1024]{1,0:T(8,128)(2,1)}, u32[]{:S(2)}) copy-start(bf16[2048,1024]{1,0:T(8,128)(2,1)} %cot_ref.1) | copy-start | bytes 12582916
  148.5 1.2 copy-start.2
  149.7 0.7 copy-start.3
  150.4 0.7 copy-start.4

commit v4 on v3

--- a/solution.py
+++ b/solution.py
@@ -155,18 +155,20 @@
         self.a = lax.rem(self.me // self.sa, 4)
         self.b = lax.rem(self.me // self.sb, 4)
         self.sibling = self.me + 1 - 2 * self.c
+        self.on_a = [lax.rem(self.a + i, 4) * self.sa for i in range(4)]
+        self.on_b = [lax.rem(self.b + j, 4) * self.sb for j in range(4)]
+
+    def first(self, i):
+        return self.on_a[i] if isinstance(i, int) else lax.rem(self.a + i, 4) * self.sa
+
+    def second(self, j):
+        return self.on_b[j] if isinstance(j, int) else lax.rem(self.b + j, 4) * self.sb
 
     def mine(self, i, j):
-        return (
-            lax.rem(self.a + i, 4) * self.sa + lax.rem(self.b + j, 4) * self.sb + self.c
-        )
+        return self.first(i) + self.second(j) + self.c
 
     def theirs(self, i, j):
-        return (
-            lax.rem(self.b + i, 4) * self.sb
-            + lax.rem(self.a + j, 4) * self.sa
-            + 1 - self.c
-        )
+        return self.second(i) + self.first(j) + 1 - self.c
 
 
 def key_block(kv, block):
@@ -184,8 +186,8 @@
 def sublayer_kernel(
     idx_ref, dest_ref, count_ref, gain_ref, rw_ref,
     tok_hbm, cot_hbm, wq_hbm, wk_hbm, wv_hbm, wo_hbm,
-    got, source_ref, factor_ref,
-    tok, cot, wq, wkv, wo, pick, sendx, senddy, gotx, gotdy, sendm, gotm, sendf, gotf,
+    got, source_ref,
+    tok, cot, wq, wkv, wo, pick, sendx, senddy, gotx, gotdy, sendm, gotm,
     fullx, fulldy, place, qpos, qkv, sums, q4, qt4, g4, gt4, acc, den, lden, delta,
     inv_col, router_col, dq, dqb, dkv,
     kv, to_sib, from_sib, to_b, from_b, to_a, from_a, far, near, relay, arrived, stats,
@@ -202,6 +204,7 @@
     rows = ROUTED_DEV
     heads = wq.shape[1] // HEAD_DIM
     pair = slots // peers
+    parts = quarter // TILE
     right, left, across = lax.rem(m + 1, 4), lax.rem(m + 3, 4), lax.rem(m + 2, 4)
     loads = [
         pltpu.make_async_copy(src, dst, load_sem.at[n])
@@ -266,7 +269,7 @@
         lax.fori_loop(1, peers, body, 0)
         dst[me] = src[me]
 
-    send_meta(sendm, gotm, 3)
+    send_meta(sendm, gotm, 5)
 
     def pack(held, send, start, width):
         def body(n, carry):
@@ -278,12 +281,11 @@
         return pl.ds(start, width)
 
     loads[0].wait()
-    for n in range(2):
-        cols = pack(tok, sendx, n * CHUNK, CHUNK)
+    for n in range(parts):
+        cols = pack(tok, sendx, n * TILE, TILE)
         send_pairs(peers, sendx, gotx, a2a_send.at[n], a2a_recv.at[n], pair, cols)
     loads[1].wait()
-    cols = pack(cot, senddy, 0, quarter)
-    send_pairs(peers, senddy, gotdy, a2a_send.at[2], a2a_recv.at[2], pair, cols)
+    pack(cot, senddy, 0, quarter)
     source_row = jnp.sum(jnp.where(rows_i == cols_i, source, 0), axis=0, keepdims=True)
     source_ref[...] = jnp.broadcast_to(source_row, source_ref.shape)
 
@@ -296,7 +298,7 @@
         out = dot(got_rows, onehot(column == within + shift))
         return jnp.sum(jnp.where(sender, out, 0.0), axis=0, keepdims=True)
 
-    await_bytes(gotm.at[others], a2a_recv.at[3])
+    await_bytes(gotm.at[others], a2a_recv.at[5])
     got_meta = gotm[:, 0, :].astype(bf16)
     slot_in = flat(got_meta, 0)
     pos_in = flat(got_meta, pair) * 256.0 + flat(got_meta, 2 * pair)
@@ -337,28 +339,28 @@
         qkv[:, :split] += dot(scaled, wq[f, :])
         qkv[:, split:] += dot(scaled, wkv[f, :])
 
-    rings = [Ring(fullx, x_send, x_recv, 6 * n, n * CHUNK, CHUNK) for n in range(2)]
-    for n in range(2):
-        await_bytes(arrived_span(gotx, CHUNK, n * CHUNK), a2a_recv.at[n])
-        compact(gotx, fullx, n * CHUNK, CHUNK)
+    rings = [Ring(fullx, x_send, x_recv, 6 * n, n * TILE, TILE) for n in range(parts)]
+    for n in range(parts):
+        await_bytes(arrived_span(gotx, TILE, n * TILE), a2a_recv.at[n])
+        compact(gotx, fullx, n * TILE, TILE)
         rings[n].begin()
+        if n > 0:
+            rings[n - 1].forward()
+    whole_cols = pl.ds(0, quarter)
+    send_pairs(peers, senddy, gotdy, a2a_send.at[4], a2a_recv.at[4], pair, whole_cols)
     for n in range(2, 5):
         loads[n].wait()
     project(m, 0, quarter)
-    rings[0].forward()
-    rings[0].near()
-    project(left, 0, CHUNK)
-    project(right, 0, CHUNK)
-    rings[1].forward()
-    rings[0].end()
-    project(across, 0, CHUNK)
-    rings[1].near()
-    project(left, CHUNK, CHUNK)
-    project(right, CHUNK, CHUNK)
-    await_bytes(arrived_span(gotdy, quarter), a2a_recv.at[2])
-    compact(gotdy, fulldy, 0, quarter)
-    rings[1].end()
-    project(across, CHUNK, CHUNK)
+    rings[parts - 1].forward()
+    for n in range(parts):
+        rings[n].near()
+        rings[n].end()
+
+        def body(i, carry):
+            project(lax.rem(m + i, 4), n * TILE, TILE)
+            return carry
+
+        lax.fori_loop(1, 4, body, 0)
 
     mean = jnp.sum(sums[0], axis=1, keepdims=True) * (1.0 / (4 * quarter))
     inv = lax.rsqrt(mean + norm_eps)
@@ -369,6 +371,8 @@
     split = heads * HEAD_DIM
     kv[me, :rows, :] = (qkv[:, split:] * inv).astype(bf16)
 
+    await_bytes(arrived_span(gotdy, quarter), a2a_recv.at[4])
+    compact(gotdy, fulldy, 0, quarter)
     half = rows // 2
     whole, top, low = pl.ds(0, rows + 16), pl.ds(0, half), pl.ds(half, half + 16)
 
@@ -407,76 +411,76 @@
             acc[r] += dot(w.astype(bf16), values)
 
     def order(t):
-        a = (t + 12) // 16
-        b = (t + 4) // 16
+        if isinstance(t, int):
+            t = max(0, t)
+            u = t if t < 4 else (t - 4) // 2 if t < 12 else t - 12
+            return [0, 1, 3, 2][u], 0 if t < 4 else 1 + 2 * (t % 2) if t < 12 else 2
+        a = lax.div(t + 12, 16)
+        b = lax.div(t + 4, 16)
         u = (1 - a) * t + (a - b) * lax.div(t - 4, 2) + b * (t - 12)
-        i = u + (u // 2) * (1 - 2 * lax.rem(u, 2))
+        i = u + lax.div(u, 2) * (1 - 2 * lax.rem(u, 2))
         j = (a - b) * (1 + 2 * lax.rem(t, 2)) + 2 * b
         return i, j
 
     def take(t):
-        block = at.mine(*order(t))
+        i, j = order(t)
+        block = at.mine(i, j)
         receive(block)
-
-        @pl.when(t == 1)
-        def _():
-            send(block, at.mine(3, 0), low)
-
-        @pl.when(t == 2)
-        def _():
-            send(block, at.mine(1, 0), top)
-
-        @pl.when(t < 4)
-        def _():
-            send(block, at.mine(0, 1))
-            send(block, at.mine(0, 3))
-
-        @pl.when(jnp.logical_and(t >= 4, t < 12))
-        def _():
-            @pl.when(lax.rem(t, 2) == 0)
+        if isinstance(t, int):
+            if t == 1:
+                send(block, at.mine(3, 0), low)
+            if t == 2:
+                send(block, at.mine(1, 0), top)
+            if t < 4:
+                send(block, at.mine(0, 1))
+                send(block, at.mine(0, 3))
+        else:
+
+            @pl.when(t < 4)
+            def _():
+                send(block, at.mine(0, 1))
+                send(block, at.mine(0, 3))
+
+            @pl.when(jnp.logical_and(t >= 4, j == 1))
             def _():
                 send(block, at.mine(0, 3), low)
 
-            @pl.when(lax.rem(t, 2) == 1)
+            @pl.when(j == 3)
             def _():
                 send(block, at.mine(0, 1), top)
 
         send(block, at.sibling)
         return block
 
-    def pair_of(t):
-        a, b = at.theirs(*order(t)), at.theirs(*order(t + 1))
-        receive(a)
-        receive(b)
-        return a, b
+    def other(t):
+        block = at.theirs(*order(t))
+        receive(block)
+        return block
 
     process(me)
     for h in range(heads):
         r = slice(h * rows, (h + 1) * rows)
         qt4[:, r] = q4[r, :].T
+    blocks = [take(1), take(2), other(0)]
+    for block in blocks:
+        process(block)
 
     def step(s, carry):
         t = 1 + 2 * s
-        a = take(t)
-        b = take(t + 1)
+        blocks = [take(t), take(t + 1), other(t - 2), other(t - 1)]
 
         @pl.when(s == 2)
         def _():
             dy_ring.forward()
 
-        process(a)
-        process(b)
-        c, d = pair_of(t - 1)
-        process(c)
-        process(d)
+        for block in blocks:
+            process(block)
         return carry
 
-    lax.fori_loop(0, 7, step, 0)
-    a = take(15)
-    process(a)
-    c, d = pair_of(14)
-    process(c)
-    process(d)
+    lax.fori_loop(1, 7, step, 0)
+    blocks = [other(13), other(14), take(15), other(15)]
+    for block in blocks:
+        process(block)
 
     loads[5].wait()
     dy_ring.near()
@@ -597,6 +601,10 @@
         dqb[:, h * HEAD_DIM : (h + 1) * HEAD_DIM] = (dq[r] * SCALE).astype(bf16)
 
     chunks = quarter // TILE
+    stat = jnp.sum(dqb[...].astype(f32) * qkv[:, :split], axis=1, keepdims=True)
+    stat = stat + jnp.sum(dkv[...].astype(f32) * qkv[:, split:], axis=1, keepdims=True)
+    stats[1, m] = jnp.broadcast_to(as_row(stat), stats.shape[2:])
+    send_stats(1)
 
     def contribution(block, n):
         f = span_of(block * quarter + n * TILE, TILE)
@@ -625,6 +633,19 @@
         copies[n].append(rs(near.at[1, low, cols], arrived.at[1, low, cols], n, 5, left))
         copies[n][5].start()
 
+    back = sendx
+
+    def finish_part(n):
+        cols = pl.ds(n * TILE, TILE)
+        f = span_of(m * quarter + n * TILE, TILE)
+        own = contribution(m, n)
+        for c in copies[n][2:]:
+            c.wait_recv()
+        own = own + arrived[0, :, cols].astype(f32) + arrived[1, :, cols].astype(f32)
+        branch = inv * own - fullx[:, f].astype(f32) * factor + rw_ref[:, f] * router_grad
+        back[:, cols] = dot(place[...], branch.astype(bf16), TN).astype(bf16)
+        send_pairs(peers, back, got, back_send.at[n], back_recv.at[n], pair, cols)
+
     for n in range(chunks):
         cols = pl.ds(n * TILE, TILE)
         far[:, cols] = contribution(across, n).astype(bf16)
@@ -639,53 +660,25 @@
         fourth = rs(near.at[1, top, cols], arrived.at[1, top, cols], n, 3, left)
         fourth.start()
         copies.append([first, second, third, fourth])
+        if n == 0:
+            router_grad = take_stats(0)
+            inv = inv_col[:, 0:1]
+            for k in range(parts):
+                await_bytes(arrived_span(sendx, TILE, k * TILE), a2a_send.at[k])
+            factor = inv * inv * inv * take_stats(1) * (1.0 / (4 * quarter))
         if n > 0:
             hand_over(n - 1)
+        if n > 1:
+            finish_part(n - 2)
     hand_over(chunks - 1)
-
-    router_grad = take_stats(0)
-    await_bytes(arrived_span(sendx, CHUNK), a2a_send.at[0])
-    await_bytes(arrived_span(sendx, CHUNK, CHUNK), a2a_send.at[1])
-    back = sendx
-    inv = inv_col[:, 0:1]
-    stat = jnp.zeros((rows, 128), f32)
-    for n in range(chunks):
-        cols = pl.ds(n * TILE, TILE)
-        f = span_of(m * quarter + n * TILE, TILE)
-        own = contribution(m, n)
-        for c in copies[n][2:]:
-            c.wait_recv()
-        own = own + arrived[0, :, cols].astype(f32) + arrived[1, :, cols].astype(f32)
-        stat = stat + lane_parts(fullx[:, f].astype(f32) * own)
-        branch = (inv * own + rw_ref[:, f] * router_grad).astype(bf16)
-        back[:, cols] = dot(place[...], branch, TN).astype(bf16)
-        send_pairs(peers, back, got, back_send.at[n], back_recv.at[n], pair, cols)
-
-    stats[1, m] = jnp.broadcast_to(
-        as_row(jnp.sum(stat, axis=1, keepdims=True)), stats.shape[2:]
-    )
-    send_stats(1)
-    factor = inv * inv * inv * take_stats(1) * (1.0 / (4 * quarter))
-    rest = jnp.sum(jnp.where(place[...].astype(f32) > 0.5, factor, 0.0), axis=0, keepdims=True)
-    slot_lane = jnp.bitwise_and(iota((1, slots), 1), pair - 1)
-    meta = jnp.zeros((peers, 128), f32)
-    for n in range(3):
-        piece = rest.astype(bf16).astype(f32)
-        rest = rest - piece
-        meta = meta + spread(sender, piece, slot_lane, n * pair)
-    sendf[...] = jnp.broadcast_to(meta[:, None, :], sendf.shape)
-    send_meta(sendf, gotf, 4)
-    await_bytes(gotf.at[others], a2a_recv.at[4])
-    got_meta = gotf[:, 0, :].astype(bf16)
-    factor_row = flat(got_meta, 0) + flat(got_meta, pair) + flat(got_meta, 2 * pair)
-    factor_ref[...] = jnp.broadcast_to(factor_row, factor_ref.shape)
+    finish_part(chunks - 2)
+    finish_part(chunks - 1)
 
     for n in range(chunks):
         await_bytes(arrived_span(got, TILE, n * TILE), back_recv.at[n])
         await_bytes(arrived_span(back, TILE, n * TILE), back_send.at[n])
-    await_bytes(arrived_span(senddy, quarter), a2a_send.at[2])
-    await_bytes(sendm.at[others], a2a_send.at[3])
-    await_bytes(sendf.at[others], a2a_send.at[4])
+    await_bytes(arrived_span(senddy, quarter), a2a_send.at[4])
+    await_bytes(sendm.at[others], a2a_send.at[5])
     for ring in rings:
         ring.sent()
     dy_ring.sent()
@@ -722,11 +715,10 @@
     return pl.pallas_call(
         sublayer_kernel,
         in_specs=[vmem, vmem, pl.BlockSpec(memory_space=pltpu.SMEM), vmem, vmem] + [hbm] * 6,
-        out_specs=[vmem] * 3,
+        out_specs=[vmem] * 2,
         out_shape=[
             shape((slots, quarter), bf16),
             shape((8, slots), jnp.int32),
-            shape((8, slots), f32),
         ],
         scratch_shapes=[
             ram((tok_rows, quarter), bf16), ram((tok_rows, quarter), bf16),
@@ -734,7 +726,6 @@
             ram((slots, tok_rows), bf16),
             ram((slots, quarter), bf16), ram((slots, quarter), bf16),
             ram((slots, quarter), bf16), ram((slots, quarter), bf16),
-            ram((peers, 8, 128), f32), ram((peers, 8, 128), f32),
             ram((peers, 8, 128), f32), ram((peers, 8, 128), f32),
             ram((rows, width), bf16), ram((rows, width), bf16),
             ram((rows, slots), bf16), ram((rows, 128), f32),
@@ -751,7 +742,7 @@
             ram((rows, quarter), bf16), ram((2, rows, quarter), bf16),
             ram((2, rows // 2, quarter), bf16), ram((2, rows, quarter), bf16),
             ram((2, 4, 8, rows), f32),
-            dma((6,)), dma((5,)), dma((5,)), dma((12,)), dma((12,)), dma((6,)), dma((6,)),
+            dma((6,)), dma((6,)), dma((6,)), dma((24,)), dma((24,)), dma((6,)), dma((6,)),
             dma, dma((peers,)),
             dma((3,)), dma((16,)), dma((16,)), dma((4,)), dma((24,)), dma((24,)),
             dma((4,)), dma((4,)), dma((2,)), dma((2,)),
@@ -766,18 +757,16 @@
     )
 
 
-def final_kernel(tok_ref, cot_ref, got_ref, source_ref, factor_ref, out_ref):
-    block, slots = tok_ref.shape[0], got_ref.shape[0]
+def final_kernel(cot_ref, got_ref, source_ref, out_ref):
+    block, slots = cot_ref.shape[0], got_ref.shape[0]
     first = pl.program_id(0) * block
-    put = iota((block, slots), 0) + first == source_ref[0:1, :]
-    factor = jnp.sum(jnp.where(put, factor_ref[0:1, :], 0.0), axis=1, keepdims=True)
-    moved = dot(onehot(put), got_ref[...])
-    out = cot_ref[...].astype(jnp.float32) + moved
-    out_ref[...] = (out - tok_ref[...].astype(jnp.float32) * factor).astype(jnp.bfloat16)
-
-
-def finish(tokens, cotangent, got, source, factor):
-    tok_rows, quarter = tokens.shape
+    put = onehot(iota((block, slots), 0) + first == source_ref[0:1, :])
+    out = cot_ref[...].astype(jnp.float32) + dot(put, got_ref[...])
+    out_ref[...] = out.astype(jnp.bfloat16)
+
+
+def finish(cotangent, got, source):
+    tok_rows, quarter = cotangent.shape
     block = pl.BlockSpec((256, quarter), lambda i: (i, 0))
 
     def whole(array):
@@ -786,14 +775,14 @@
     return pl.pallas_call(
         final_kernel,
         grid=(tok_rows // 256,),
-        in_specs=[block, block, whole(got), whole(source), whole(factor)],
+        in_specs=[block, whole(got), whole(source)],
         out_specs=block,
-        out_shape=jax.ShapeDtypeStruct(tokens.shape, jnp.bfloat16),
+        out_shape=jax.ShapeDtypeStruct(cotangent.shape, jnp.bfloat16),
         compiler_params=pltpu.CompilerParams(
-            dimension_semantics=("arbitrary",), vmem_limit_bytes=32 * MIB
+            dimension_semantics=("arbitrary",), vmem_limit_bytes=VMEM_LIMIT
         ),
         name="add_branch",
-    )(tokens, cotangent, got, source, factor)
+    )(cotangent, got, source)
 
 
 def on_device(
@@ -809,7 +798,7 @@
     routed_count,
     routed_dest,
 ):
-    got, source, factor = sublayer(
+    got, source = sublayer(
         tokens,
         cotangent,
         norm_gain[None, :],
@@ -822,7 +811,7 @@
         routed_count,
         routed_dest,
     )
-    return finish(tokens, cotangent, got, source, factor)
+    return finish(cotangent, got, source)
 
 
 def solution(mesh):

time: 157 us -> 144 us (0.917)
  local copies, waits for them, and re-layouts: 7.03 us -> 0 us
  Pallas kernels: 149 us -> 143 us
    pallas_call x1, Pallas kernels: 143 us -> 135 us  [sublayer(): pl.pallas_call(sublayer_kernel, in_specs=[vmem, vmem, pl.BlockSpec(memory...]
    unnamed x10 -> x0, local copies, waits for them, and re-layouts: 7.03 us -> none
    pallas_call x1, Pallas kernels: 5.53 us -> 8.4 us  [finish(): pl.pallas_call(final_kernel, grid=(tok_rows // 256,), in_specs=[block, wh...]
where the time goes in v4:
time: 144 us
  Pallas kernels  143 us (99%)
    pallas_call x1, Pallas kernels, sublayer(): pl.pallas_call(sublayer_kernel, in_specs=[vmem, vmem, pl.BlockSpec(memory...  135 us
    pallas_call x1, Pallas kernels, finish(): pl.pallas_call(final_kernel, grid=(tok_rows // 256,), in_specs=[block, wh...  8.4 us

profile of v4, /device:TPU:1, one launch (start us, length us, event | category | flops | bytes accessed | tf_op | source)
XLA Modules:
  0.0 143.8 jit_solution(5988849888006791838)
XLA Ops:
  0.7 134.7 %sublayer.1 = (bf16[512,1024]{1,0:T(8,128)(2,1)}, s32[8,512]{1,0:T(8,128)}) custom-call(s32[1,512]{1,0:T(1,128)} %idx_ref.1, s32[1,512]{1,0:T(1,128)} %dest_ref.1, s32[1]{0:T(128)S(6)} %copy.12.count_ref, f32[1,4096]{1,0:T(1,128)} %bitcast.2, f32[1,4096]{1,0:T(1,128)} %bitcast.3, bf16[2048,1024]{1,0:T(8,128)(2,1)} %tok_hbm.1, bf16[2048,1024]{1,0:T(8,128)(2,1)} %cot_ref.1, ...), custom_call_target="tpu_custom_call" | custom-call | tf_op jit(solution)/shard_map/sublayer/pallas_call | solution.py:715
  135.4 8.4 %add_branch.1 = bf16[2048,1024]{1,0:T(8,128)(2,1)} custom-call(bf16[2048,1024]{1,0:T(8,128)(2,1)} %cot_ref.1, bf16[512,1024]{1,0:T(8,128)(2,1)} %get-tuple-element.7.got_ref, s32[8,512]{1,0:T(8,128)} %get-tuple-element.8.source_ref), custom_call_target="tpu_custom_call" | custom-call | tf_op jit(solution)/shard_map/add_branch/pallas_call | solution.py:775

commit v5 on v4

--- a/solution.py
+++ b/solution.py
@@ -105,6 +105,24 @@
         self.move(self.right, self.low, 1, self.left).wait_recv()
         self.move(self.right, self.low, 5, self.left).start()
 
+    def whole(self, block, k, to):
+        every = pl.ds(0, self.full.shape[0])
+        return self.move(block, every, k, to)
+
+    def direct(self):
+        self.whole(self.m, 0, self.right).start()
+        self.whole(self.m, 1, self.left).start()
+        self.whole(self.m, 4, self.far).start()
+
+    def direct_end(self):
+        self.whole(self.left, 0, self.right).wait_recv()
+        self.whole(self.right, 1, self.left).wait_recv()
+        self.whole(self.far, 4, self.far).wait_recv()
+
+    def direct_sent(self):
+        for k in (0, 1, 4):
+            self.whole(self.m, k, self.right).wait_send()
+
     def near(self):
         self.move(self.left, self.low, 2, self.right).wait_recv()
         self.move(self.right, self.top, 3, self.left).wait_recv()
@@ -180,6 +198,7 @@
 
 
 CHUNK = 512
+FINAL_ROWS = 512
 TILE = 256
 
 
@@ -219,8 +238,7 @@
             ]
         )
     ]
-    for load in loads:
-        load.start()
+    loads[0].start()
     greet("seq", peers)
     greet("mp", 4)
 
@@ -281,6 +299,8 @@
         return pl.ds(start, width)
 
     loads[0].wait()
+    for load in loads[1:]:
+        load.start()
     for n in range(parts):
         cols = pack(tok, sendx, n * TILE, TILE)
         send_pairs(peers, sendx, gotx, a2a_send.at[n], a2a_recv.at[n], pair, cols)
@@ -348,10 +368,10 @@
             rings[n - 1].forward()
     whole_cols = pl.ds(0, quarter)
     send_pairs(peers, senddy, gotdy, a2a_send.at[4], a2a_recv.at[4], pair, whole_cols)
+    rings[parts - 1].forward()
     for n in range(2, 5):
         loads[n].wait()
     project(m, 0, quarter)
-    rings[parts - 1].forward()
     for n in range(parts):
         rings[n].near()
         rings[n].end()
@@ -371,8 +391,6 @@
     split = heads * HEAD_DIM
     kv[me, :rows, :] = (qkv[:, split:] * inv).astype(bf16)
 
-    await_bytes(arrived_span(gotdy, quarter), a2a_recv.at[4])
-    compact(gotdy, fulldy, 0, quarter)
     half = rows // 2
     whole, top, low = pl.ds(0, rows + 16), pl.ds(0, half), pl.ds(half, half + 16)
 
@@ -386,10 +404,11 @@
     send(me, at.mine(1, 0))
     send(me, at.mine(3, 0))
     send(me, at.sibling)
-    send(me, at.mine(0, 1))
-    send(me, at.mine(0, 3))
-    dy_ring = Ring(fulldy, d_send, d_recv, 0, 0, quarter)
-    dy_ring.begin()
+    dy_rings = [Ring(fulldy, d_send, d_recv, 6 * n, n * TILE, TILE) for n in range(parts)]
+    await_bytes(arrived_span(gotdy, quarter), a2a_recv.at[4])
+    compact(gotdy, fulldy, 0, quarter)
+    dy_rings[0].begin()
+    dy_rings[1].begin()
     for h in range(heads):
         part = (qkv[:, h * HEAD_DIM : (h + 1) * HEAD_DIM] * inv).astype(bf16)
         q4[h * rows : (h + 1) * rows, :] = part
@@ -431,6 +450,9 @@
                 send(block, at.mine(3, 0), low)
             if t == 2:
                 send(block, at.mine(1, 0), top)
+            if t == 1:
+                send(me, at.mine(0, 1))
+                send(me, at.mine(0, 3))
             if t < 4:
                 send(block, at.mine(0, 1))
                 send(block, at.mine(0, 3))
@@ -469,9 +491,12 @@
         t = 1 + 2 * s
         blocks = [take(t), take(t + 1), other(t - 2), other(t - 1)]
 
-        @pl.when(s == 2)
+        @pl.when(s == 1)
         def _():
-            dy_ring.forward()
+            for ring in dy_rings[:2]:
+                ring.forward()
+            for ring in dy_rings[2:]:
+                ring.direct()
 
         for block in blocks:
             process(block)
@@ -483,8 +508,11 @@
         process(block)
 
     loads[5].wait()
-    dy_ring.near()
-    dy_ring.end()
+    for ring in dy_rings[:2]:
+        ring.near()
+        ring.end()
+    for ring in dy_rings[2:]:
+        ring.direct_end()
     router = router_col[...]
     dots = jnp.zeros((rows, 1), f32)
     for n in range(split // TILE):
@@ -601,11 +629,6 @@
         dqb[:, h * HEAD_DIM : (h + 1) * HEAD_DIM] = (dq[r] * SCALE).astype(bf16)
 
     chunks = quarter // TILE
-    stat = jnp.sum(dqb[...].astype(f32) * qkv[:, :split], axis=1, keepdims=True)
-    stat = stat + jnp.sum(dkv[...].astype(f32) * qkv[:, split:], axis=1, keepdims=True)
-    stats[1, m] = jnp.broadcast_to(as_row(stat), stats.shape[2:])
-    send_stats(1)
-
     def contribution(block, n):
         f = span_of(block * quarter + n * TILE, TILE)
         total = dot(dqb[...], wq[f, :], NT) + dot(dkv[...], wkv[f, :], NT)
@@ -646,7 +669,7 @@
         back[:, cols] = dot(place[...], branch.astype(bf16), TN).astype(bf16)
         send_pairs(peers, back, got, back_send.at[n], back_recv.at[n], pair, cols)
 
-    for n in range(chunks):
+    def issue(n):
         cols = pl.ds(n * TILE, TILE)
         far[:, cols] = contribution(across, n).astype(bf16)
         first = rs(far.at[top, cols], relay.at[0, :, cols], n, 0, right)
@@ -660,18 +683,24 @@
         fourth = rs(near.at[1, top, cols], arrived.at[1, top, cols], n, 3, left)
         fourth.start()
         copies.append([first, second, third, fourth])
-        if n == 0:
-            router_grad = take_stats(0)
-            inv = inv_col[:, 0:1]
-            for k in range(parts):
-                await_bytes(arrived_span(sendx, TILE, k * TILE), a2a_send.at[k])
-            factor = inv * inv * inv * take_stats(1) * (1.0 / (4 * quarter))
-        if n > 0:
-            hand_over(n - 1)
-        if n > 1:
-            finish_part(n - 2)
-    hand_over(chunks - 1)
-    finish_part(chunks - 2)
+
+    issue(0)
+    stat = jnp.sum(dqb[...].astype(f32) * qkv[:, :split], axis=1, keepdims=True)
+    stat = stat + jnp.sum(dkv[...].astype(f32) * qkv[:, split:], axis=1, keepdims=True)
+    stats[1, m] = jnp.broadcast_to(as_row(stat), stats.shape[2:])
+    send_stats(1)
+    issue(1)
+    router_grad = take_stats(0)
+    inv = inv_col[:, 0:1]
+    for k in range(parts):
+        await_bytes(arrived_span(sendx, TILE, k * TILE), a2a_send.at[k])
+    hand_over(0)
+    factor = inv * inv * inv * take_stats(1) * (1.0 / (4 * quarter))
+    for n in range(1, chunks):
+        if n + 1 < chunks:
+            issue(n + 1)
+        hand_over(n)
+        finish_part(n - 1)
     finish_part(chunks - 1)
 
     for n in range(chunks):
@@ -679,9 +708,10 @@
         await_bytes(arrived_span(back, TILE, n * TILE), back_send.at[n])
     await_bytes(arrived_span(senddy, quarter), a2a_send.at[4])
     await_bytes(sendm.at[others], a2a_send.at[5])
-    for ring in rings:
+    for ring in rings + dy_rings[:2]:
         ring.sent()
-    dy_ring.sent()
+    for ring in dy_rings[2:]:
+        ring.direct_sent()
     for group in copies:
         for c in group:
             c.wait_send()
@@ -742,7 +772,7 @@
             ram((rows, quarter), bf16), ram((2, rows, quarter), bf16),
             ram((2, rows // 2, quarter), bf16), ram((2, rows, quarter), bf16),
             ram((2, 4, 8, rows), f32),
-            dma((6,)), dma((6,)), dma((6,)), dma((24,)), dma((24,)), dma((6,)), dma((6,)),
+            dma((6,)), dma((6,)), dma((6,)), dma((24,)), dma((24,)), dma((24,)), dma((24,)),
             dma, dma((peers,)),
             dma((3,)), dma((16,)), dma((16,)), dma((4,)), dma((24,)), dma((24,)),
             dma((4,)), dma((4,)), dma((2,)), dma((2,)),
@@ -757,30 +787,46 @@
     )
 
 
-def final_kernel(cot_ref, got_ref, source_ref, out_ref):
-    block, slots = cot_ref.shape[0], got_ref.shape[0]
-    first = pl.program_id(0) * block
-    put = onehot(iota((block, slots), 0) + first == source_ref[0:1, :])
-    out = cot_ref[...].astype(jnp.float32) + dot(put, got_ref[...])
-    out_ref[...] = out.astype(jnp.bfloat16)
+def final_kernel(cot_hbm, got_hbm, source_ref, out_hbm, cot, got, out, loads, stores):
+    block, slots = FINAL_ROWS, got.shape[0]
+    steps = cot.shape[0] // block
+    got_load = pltpu.make_async_copy(got_hbm, got, loads.at[steps])
+    got_load.start()
+
+    def copy(n, src, dst, sems):
+        rows = pl.ds(n * block, block)
+        return pltpu.make_async_copy(src.at[rows], dst.at[rows], sems.at[n])
+
+    for n in range(steps):
+        copy(n, cot_hbm, cot, loads).start()
+    got_load.wait()
+    for n in range(steps):
+        rows = pl.ds(n * block, block)
+        put = onehot(iota((block, slots), 0) + n * block == source_ref[0:1, :])
+        copy(n, cot_hbm, cot, loads).wait()
+        total = cot[rows, :].astype(jnp.float32) + dot(put, got[...])
+        out[rows, :] = total.astype(jnp.bfloat16)
+        copy(n, out, out_hbm, stores).start()
+    for n in range(steps):
+        copy(n, out, out_hbm, stores).wait()
 
 
 def finish(cotangent, got, source):
-    tok_rows, quarter = cotangent.shape
-    block = pl.BlockSpec((256, quarter), lambda i: (i, 0))
-
-    def whole(array):
-        return pl.BlockSpec(array.shape, lambda i: (0, 0))
-
+    hbm = pl.BlockSpec(memory_space=pl.ANY)
+    steps = cotangent.shape[0] // FINAL_ROWS
     return pl.pallas_call(
         final_kernel,
-        grid=(tok_rows // 256,),
-        in_specs=[block, whole(got), whole(source)],
-        out_specs=block,
+        in_specs=[hbm, hbm, pl.BlockSpec(memory_space=pltpu.VMEM)],
+        out_specs=hbm,
         out_shape=jax.ShapeDtypeStruct(cotangent.shape, jnp.bfloat16),
-        compiler_params=pltpu.CompilerParams(
-            dimension_semantics=("arbitrary",), vmem_limit_bytes=VMEM_LIMIT
-        ),
+        scratch_shapes=[
+            pltpu.VMEM(cotangent.shape, jnp.bfloat16),
+            pltpu.VMEM(got.shape, jnp.bfloat16),
+            pltpu.VMEM(cotangent.shape, jnp.bfloat16),
+            pltpu.SemaphoreType.DMA((steps + 1,)),
+            pltpu.SemaphoreType.DMA((steps,)),
+        ],
+        compiler_params=pltpu.CompilerParams(vmem_limit_bytes=VMEM_LIMIT),
         name="add_branch",
     )(cotangent, got, source)
 

time: 144 us -> 143 us (level)
    pallas_call x1, Pallas kernels: 8.4 us -> 6.24 us  [finish(): pl.pallas_call(final_kernel, in_specs=[hbm, hbm, pl.BlockSpec(memory_spac...]
where the time goes in v5:
time: 143 us; the launch traced here: 142 us
  Pallas kernels  142 us (99%)
    pallas_call x1, Pallas kernels, sublayer(): pl.pallas_call(sublayer_kernel, in_specs=[vmem, vmem, pl.BlockSpec(memory...  135 us
    pallas_call x1, Pallas kernels, finish(): pl.pallas_call(final_kernel, in_specs=[hbm, hbm, pl.BlockSpec(memory_spac...  6.24 us

profile of v5, /device:TPU:1, one launch (start us, length us, event | category | flops | bytes accessed | tf_op | source)
XLA Modules:
  0.0 142.4 jit_solution(6210597408661548628)
XLA Ops:
  0.7 135.3 %sublayer.1 = (bf16[512,1024]{1,0:T(8,128)(2,1)}, s32[8,512]{1,0:T(8,128)}) custom-call(s32[1,512]{1,0:T(1,128)} %idx_ref.1, s32[1,512]{1,0:T(1,128)} %dest_ref.1, s32[1]{0:T(128)S(6)} %copy.12.count_ref, f32[1,4096]{1,0:T(1,128)} %bitcast.2, f32[1,4096]{1,0:T(1,128)} %bitcast.3, bf16[2048,1024]{1,0:T(8,128)(2,1)} %tok_hbm.1, bf16[2048,1024]{1,0:T(8,128)(2,1)} %cot_hbm.3, ...), custom_call_target="tpu_custom_call" | custom-call | tf_op jit(solution)/shard_map/sublayer/pallas_call | solution.py:745
  136.0 6.2 %add_branch.1 = bf16[2048,1024]{1,0:T(8,128)(2,1)} custom-call(bf16[2048,1024]{1,0:T(8,128)(2,1)} %cot_hbm.3, bf16[512,1024]{1,0:T(8,128)(2,1)} %get-tuple-element.7.got_hbm, s32[8,512]{1,0:T(8,128)} %get-tuple-element.8.source_ref), custom_call_target="tpu_custom_call" | custom-call | tf_op jit(solution)/shard_map/add_branch/pallas_call | solution.py:817

commit v6 on v5

--- a/solution.py
+++ b/solution.py
@@ -105,24 +105,6 @@
         self.move(self.right, self.low, 1, self.left).wait_recv()
         self.move(self.right, self.low, 5, self.left).start()
 
-    def whole(self, block, k, to):
-        every = pl.ds(0, self.full.shape[0])
-        return self.move(block, every, k, to)
-
-    def direct(self):
-        self.whole(self.m, 0, self.right).start()
-        self.whole(self.m, 1, self.left).start()
-        self.whole(self.m, 4, self.far).start()
-
-    def direct_end(self):
-        self.whole(self.left, 0, self.right).wait_recv()
-        self.whole(self.right, 1, self.left).wait_recv()
-        self.whole(self.far, 4, self.far).wait_recv()
-
-    def direct_sent(self):
-        for k in (0, 1, 4):
-            self.whole(self.m, k, self.right).wait_send()
-
     def near(self):
         self.move(self.left, self.low, 2, self.right).wait_recv()
         self.move(self.right, self.top, 3, self.left).wait_recv()
@@ -162,6 +144,12 @@
     size = row.shape[1]
     eye = iota((size, size), 0) == iota((size, size), 1)
     return jnp.sum(jnp.where(eye, row, 0.0), axis=1, keepdims=True)
+
+
+def when(condition):
+    if isinstance(condition, bool):
+        return lambda f: f() if condition else None
+    return pl.when(condition)
 
 
 class Place:
@@ -306,6 +294,8 @@
         send_pairs(peers, sendx, gotx, a2a_send.at[n], a2a_recv.at[n], pair, cols)
     loads[1].wait()
     pack(cot, senddy, 0, quarter)
+    whole_cols = pl.ds(0, quarter)
+    send_pairs(peers, senddy, gotdy, a2a_send.at[4], a2a_recv.at[4], pair, whole_cols)
     source_row = jnp.sum(jnp.where(rows_i == cols_i, source, 0), axis=0, keepdims=True)
     source_ref[...] = jnp.broadcast_to(source_row, source_ref.shape)
 
@@ -366,15 +356,20 @@
         rings[n].begin()
         if n > 0:
             rings[n - 1].forward()
-    whole_cols = pl.ds(0, quarter)
-    send_pairs(peers, senddy, gotdy, a2a_send.at[4], a2a_recv.at[4], pair, whole_cols)
     rings[parts - 1].forward()
     for n in range(2, 5):
         loads[n].wait()
     project(m, 0, quarter)
+    dy_rings = [Ring(fulldy, d_send, d_recv, 6 * n, n * TILE, TILE) for n in range(parts)]
     for n in range(parts):
+        if n == parts - 1:
+            await_bytes(arrived_span(gotdy, quarter), a2a_recv.at[4])
+            compact(gotdy, fulldy, 0, quarter)
         rings[n].near()
         rings[n].end()
+        if n == parts - 1:
+            for ring in dy_rings:
+                ring.begin()
 
         def body(i, carry):
             project(lax.rem(m + i, 4), n * TILE, TILE)
@@ -404,11 +399,6 @@
     send(me, at.mine(1, 0))
     send(me, at.mine(3, 0))
     send(me, at.sibling)
-    dy_rings = [Ring(fulldy, d_send, d_recv, 6 * n, n * TILE, TILE) for n in range(parts)]
-    await_bytes(arrived_span(gotdy, quarter), a2a_recv.at[4])
-    compact(gotdy, fulldy, 0, quarter)
-    dy_rings[0].begin()
-    dy_rings[1].begin()
     for h in range(heads):
         part = (qkv[:, h * HEAD_DIM : (h + 1) * HEAD_DIM] * inv).astype(bf16)
         q4[h * rows : (h + 1) * rows, :] = part
@@ -491,12 +481,11 @@
         t = 1 + 2 * s
         blocks = [take(t), take(t + 1), other(t - 2), other(t - 1)]
 
-        @pl.when(s == 1)
-        def _():
-            for ring in dy_rings[:2]:
-                ring.forward()
-            for ring in dy_rings[2:]:
-                ring.direct()
+        for n in range(parts):
+
+            @pl.when(s == n + 1)
+            def _():
+                dy_rings[n].forward()
 
         for block in blocks:
             process(block)
@@ -508,11 +497,9 @@
         process(block)
 
     loads[5].wait()
-    for ring in dy_rings[:2]:
+    for ring in dy_rings:
         ring.near()
         ring.end()
-    for ring in dy_rings[2:]:
-        ring.direct_end()
     router = router_col[...]
     dots = jnp.zeros((rows, 1), f32)
     for n in range(split // TILE):
@@ -570,7 +557,7 @@
     def pass_on(k, late, i, j):
         await_bytes(from_sib.at[k], sib_recv.at[k])
 
-        @pl.when(late == 0)
+        @when(late == 0)
         def _():
             summed = to_b[k].astype(f32) + from_sib[k].astype(f32)
             to_b[k] = summed.astype(bf16)
@@ -580,14 +567,14 @@
                 at.mine(0, j),
             ).start()
 
-        @pl.when(late == 1)
+        @when(late == 1)
         def _():
             total = to_b[k].astype(f32) + from_sib[k].astype(f32)
             for n in range(1, 4):
                 await_bytes(from_b.at[n * 4 + i], b_recv.at[n * 4 + i])
                 total = total + from_b[n * 4 + i].astype(f32)
 
-            @pl.when(k < 15)
+            @when(k < 15)
             def _():
                 to_a[i] = total.astype(bf16)
                 slot = 4 - i
@@ -596,7 +583,7 @@
                     at.mine(i, 0),
                 ).start()
 
-            @pl.when(k == 15)
+            @when(k == 15)
             def _():
                 final = total
                 for n in range(1, 4):
@@ -604,29 +591,44 @@
                     final = final + from_a[n].astype(f32)
                 dkv[...] = final.T.astype(bf16)
 
-    def back_step(s, carry):
+    def back_places(s):
         late = s // 6
         places = []
         for n in range(2):
             k = 2 * s + n
             j = (1 + k // 4) * (1 - late)
-            i = lax.rem(k + late, 4)
+            i = (k + late) % 4
             places.append((k, late, i, j))
+        return places
+
+    def sibling_terms(places):
         for k, _, i, j in places:
             to_sib[k] = terms(at.theirs(i, j)).astype(bf16)
             remote(
                 to_sib.at[k], from_sib.at[k], sends.at[0], sib_recv.at[k], "seq", at.sibling
             ).start()
+
+    def back_step(s, carry):
+        places = back_places(s)
+        sibling_terms(places)
         for k, _, i, j in places:
             to_b[k] = terms(at.mine(i, j)).astype(bf16)
         for where in places:
             pass_on(*where)
         return carry
 
-    lax.fori_loop(0, 8, back_step, 0)
+    lax.fori_loop(0, 7, back_step, 0)
+    places = back_places(7)
+    sibling_terms(places)
+    for k, _, i, j in places:
+        to_b[k] = terms(at.mine(i, j)).astype(bf16)
+        if k == 14:
+            pass_on(*places[0])
     for h in range(heads):
         r = slice(h * rows, (h + 1) * rows)
         dqb[:, h * HEAD_DIM : (h + 1) * HEAD_DIM] = (dq[r] * SCALE).astype(bf16)
+    stat = jnp.sum(dqb[...].astype(f32) * qkv[:, :split], axis=1, keepdims=True)
+    pass_on(*places[1])
 
     chunks = quarter // TILE
     def contribution(block, n):
@@ -685,7 +687,6 @@
         copies.append([first, second, third, fourth])
 
     issue(0)
-    stat = jnp.sum(dqb[...].astype(f32) * qkv[:, :split], axis=1, keepdims=True)
     stat = stat + jnp.sum(dkv[...].astype(f32) * qkv[:, split:], axis=1, keepdims=True)
     stats[1, m] = jnp.broadcast_to(as_row(stat), stats.shape[2:])
     send_stats(1)
@@ -708,10 +709,8 @@
         await_bytes(arrived_span(back, TILE, n * TILE), back_send.at[n])
     await_bytes(arrived_span(senddy, quarter), a2a_send.at[4])
     await_bytes(sendm.at[others], a2a_send.at[5])
-    for ring in rings + dy_rings[:2]:
+    for ring in rings + dy_rings:
         ring.sent()
-    for ring in dy_rings[2:]:
-        ring.direct_sent()
     for group in copies:
         for c in group:
             c.wait_send()

time: 143 us -> 139 us (0.972)
  Pallas kernels: 142 us -> 138 us
    pallas_call x1, Pallas kernels: 135 us -> 132 us  [sublayer(): pl.pallas_call(sublayer_kernel, in_specs=[vmem, vmem, pl.BlockSpec(memory...]
where the time goes in v6:
time: 139 us
  Pallas kernels  138 us (99%)
    pallas_call x1, Pallas kernels, sublayer(): pl.pallas_call(sublayer_kernel, in_specs=[vmem, vmem, pl.BlockSpec(memory...  132 us
    pallas_call x1, Pallas kernels, finish(): pl.pallas_call(final_kernel, in_specs=[hbm, hbm, pl.BlockSpec(memory_spac...  6.23 us

profile of v6, /device:TPU:1, one launch (start us, length us, event | category | flops | bytes accessed | tf_op | source)
XLA Modules:
  0.0 138.6 jit_solution(4435995441664459756)
XLA Ops:
  0.7 131.5 %sublayer.1 = (bf16[512,1024]{1,0:T(8,128)(2,1)}, s32[8,512]{1,0:T(8,128)}) custom-call(s32[1,512]{1,0:T(1,128)} %idx_ref.1, s32[1,512]{1,0:T(1,128)} %dest_ref.1, s32[1]{0:T(128)S(6)} %copy.12.count_ref, f32[1,4096]{1,0:T(1,128)} %bitcast.2, f32[1,4096]{1,0:T(1,128)} %bitcast.3, bf16[2048,1024]{1,0:T(8,128)(2,1)} %tok_hbm.1, bf16[2048,1024]{1,0:T(8,128)(2,1)} %cot_hbm.3, ...), custom_call_target="tpu_custom_call" | custom-call | tf_op jit(solution)/shard_map/sublayer/pallas_call | solution.py:744
  132.2 6.2 %add_branch.1 = bf16[2048,1024]{1,0:T(8,128)(2,1)} custom-call(bf16[2048,1024]{1,0:T(8,128)(2,1)} %cot_hbm.3, bf16[512,1024]{1,0:T(8,128)(2,1)} %get-tuple-element.7.got_hbm, s32[8,512]{1,0:T(8,128)} %get-tuple-element.8.source_ref), custom_call_target="tpu_custom_call" | custom-call | tf_op jit(solution)/shard_map/add_branch/pallas_call | solution.py:816

commit v7 on v6

--- a/solution.py
+++ b/solution.py
@@ -186,7 +186,6 @@
 
 
 CHUNK = 512
-FINAL_ROWS = 512
 TILE = 256
 
 
@@ -398,6 +397,7 @@
 
     send(me, at.mine(1, 0))
     send(me, at.mine(3, 0))
+    send(me, at.mine(2, 0))
     send(me, at.sibling)
     for h in range(heads):
         part = (qkv[:, h * HEAD_DIM : (h + 1) * HEAD_DIM] * inv).astype(bf16)
@@ -437,10 +437,6 @@
         receive(block)
         if isinstance(t, int):
             if t == 1:
-                send(block, at.mine(3, 0), low)
-            if t == 2:
-                send(block, at.mine(1, 0), top)
-            if t == 1:
                 send(me, at.mine(0, 1))
                 send(me, at.mine(0, 3))
             if t < 4:
@@ -483,7 +479,7 @@
 
         for n in range(parts):
 
-            @pl.when(s == n + 1)
+            @pl.when(s == n + 2)
             def _():
                 dy_rings[n].forward()
 
@@ -786,50 +782,6 @@
     )
 
 
-def final_kernel(cot_hbm, got_hbm, source_ref, out_hbm, cot, got, out, loads, stores):
-    block, slots = FINAL_ROWS, got.shape[0]
-    steps = cot.shape[0] // block
-    got_load = pltpu.make_async_copy(got_hbm, got, loads.at[steps])
-    got_load.start()
-
-    def copy(n, src, dst, sems):
-        rows = pl.ds(n * block, block)
-        return pltpu.make_async_copy(src.at[rows], dst.at[rows], sems.at[n])
-
-    for n in range(steps):
-        copy(n, cot_hbm, cot, loads).start()
-    got_load.wait()
-    for n in range(steps):
-        rows = pl.ds(n * block, block)
-        put = onehot(iota((block, slots), 0) + n * block == source_ref[0:1, :])
-        copy(n, cot_hbm, cot, loads).wait()
-        total = cot[rows, :].astype(jnp.float32) + dot(put, got[...])
-        out[rows, :] = total.astype(jnp.bfloat16)
-        copy(n, out, out_hbm, stores).start()
-    for n in range(steps):
-        copy(n, out, out_hbm, stores).wait()
-
-
-def finish(cotangent, got, source):
-    hbm = pl.BlockSpec(memory_space=pl.ANY)
-    steps = cotangent.shape[0] // FINAL_ROWS
-    return pl.pallas_call(
-        final_kernel,
-        in_specs=[hbm, hbm, pl.BlockSpec(memory_space=pltpu.VMEM)],
-        out_specs=hbm,
-        out_shape=jax.ShapeDtypeStruct(cotangent.shape, jnp.bfloat16),
-        scratch_shapes=[
-            pltpu.VMEM(cotangent.shape, jnp.bfloat16),
-            pltpu.VMEM(got.shape, jnp.bfloat16),
-            pltpu.VMEM(cotangent.shape, jnp.bfloat16),
-            pltpu.SemaphoreType.DMA((steps + 1,)),
-            pltpu.SemaphoreType.DMA((steps,)),
-        ],
-        compiler_params=pltpu.CompilerParams(vmem_limit_bytes=VMEM_LIMIT),
-        name="add_branch",
-    )(cotangent, got, source)
-
-
 def on_device(
     tokens,
     cotangent,
@@ -856,7 +808,9 @@
         routed_count,
         routed_dest,
     )
-    return finish(cotangent, got, source)
+    slots = jnp.arange(cotangent.shape[0], dtype=jnp.int32)
+    put = (slots[:, None] == source[0:1]).astype(jnp.bfloat16)
+    return (cotangent.astype(jnp.float32) + dot(put, got)).astype(jnp.bfloat16)
 
 
 def solution(mesh):

time: 139 us -> 140 us (level)
  matrix products: 0 us -> 7.03 us
  Pallas kernels: 138 us -> 131 us
    dot_general x0 -> x1, matrix products: none -> 7.03 us  [dot(): return lax.dot_general(a, b, dims, preferred_element_type=jnp.float32)]
    pallas_call x1 -> x0, Pallas kernels: 6.23 us -> none  [finish(): pl.pallas_call(final_kernel, in_specs=[hbm, hbm, pl.BlockSpec(memory_spac...]
where the time goes in v7:
time: 140 us; the launch traced here: 139 us
  Pallas kernels  131 us (94%)
  matrix products  7.03 us (5%)
    pallas_call x1, Pallas kernels, sublayer(): pl.pallas_call(sublayer_kernel, in_specs=[vmem, vmem, pl.BlockSpec(memory...  131 us
    dot_general x1, matrix products, dot(): return lax.dot_general(a, b, dims, preferred_element_type=jnp.float32)  7.03 us

profile of v7, /device:TPU:1, one launch (start us, length us, event | category | flops | bytes accessed | tf_op | source)
XLA Modules:
  0.0 139.3 jit_solution(11624590964103850728)
XLA Ops:
  0.7 130.9 %sublayer.1 = (bf16[512,1024]{1,0:T(8,128)(2,1)}, s32[8,512]{1,0:T(8,128)}) custom-call(s32[1,512]{1,0:T(1,128)} %idx_ref.1, s32[1,512]{1,0:T(1,128)} %dest_ref.1, s32[1]{0:T(128)S(6)} %copy.12.count_ref, f32[1,4096]{1,0:T(1,128)} %bitcast.4, f32[1,4096]{1,0:T(1,128)} %bitcast.5, bf16[2048,1024]{1,0:T(8,128)(2,1)} %tok_hbm.1, bf16[2048,1024]{1,0:T(8,128)(2,1)} %cot_hbm.1, ...), custom_call_target="tpu_custom_call" | custom-call | tf_op jit(solution)/shard_map/sublayer/pallas_call | solution.py:740
  131.6 0.7 slice.3
  132.3 7.0 %add_convert_fusion = bf16[2048,1024]{1,0:T(8,128)(2,1)} fusion(bf16[2048,1024]{1,0:T(8,128)(2,1)} %cot_hbm.1, bf16[512,1024]{1,0:T(8,128)(2,1)} %get-tuple-element.8, s32[512]{0:T(512)S(1)} %bitcast.6), kind=kOutput, calls=%fused_computation | convolution fusion | flops 2154823680 | bytes 9439232 | tf_op jit(solution)/shard_map/dot_general | solution.py:23
